TPU v7x, 32 devices: a whole 2x2x4 slice. The times are simulated.
32 devices in a mesh: row: 8 (over y, x, core), col: 4 (over z).
Axes of the slice: x: 2, y: 2, z: 4, core: 2. Of those that a mesh axis runs over, the one named last changes fastest.
Arguments:
- query_in: bfloat16 [2048, 8192], P('row', 'col'), may hold values from -6 to 6
- key_in: bfloat16 [2048, 8192], P('row', 'col'), may hold values from -6 to 6
- value_in: bfloat16 [2048, 8192], P('row', 'col'), may hold values from -6 to 6
- filters: float32 [512, 128], P('col'), may hold values from -0.5 to 0.5
- out_weight: bfloat16 [8192, 8192], P('row', 'col'), may hold values from -0.0625 to 0.0625
- out_grad: bfloat16 [2048, 8192], P('row', 'col'), may hold values from -6 to 6
Outputs:
- mixed: bfloat16 [2048, 8192], P('row', 'col')
- query_grad: bfloat16 [2048, 8192], P('row', 'col')
- key_grad: bfloat16 [2048, 8192], P('row', 'col')
- value_grad: bfloat16 [2048, 8192], P('row', 'col')
- weight_grad: bfloat16 [8192, 8192], P('row', 'col')
- filter_grad: float32 [512, 128], P('col')
All inputs are finite; a program needn't handle non-finite values.
Results may differ from a plain program's by a relative error of at most 0.018.
Values may be sent and summed in bfloat16 or wider, within the bound.
No kernel may reach another device: no remote copies, remote signals or barrier semaphores. Data moves between devices by JAX's collectives and lax.ppermute only.
A program may use at most 192 MiB of HBM per device.

v0:
```python
import math

import jax
import jax.numpy as jnp
from jax import lax
from jax.sharding import PartitionSpec as P


def from_behind(shard, axis, by):
    size = lax.axis_size(axis)
    pairs = [(i, i + by) for i in range(size) if 0 <= i + by < size]
    return lax.ppermute(shard, axis, pairs)


def toeplitz(taps, causal):
    groups, span = taps.shape
    if causal:
        template = jnp.concatenate(
            [
                jnp.zeros((groups, 1), jnp.float32),
                taps[:, ::-1],
                jnp.zeros((groups, span), jnp.float32),
            ],
            1,
        )
    else:
        template = jnp.concatenate([taps, jnp.zeros((groups, span + 1), jnp.float32)], 1)
    tiled = jnp.tile(template, (1, span))
    return tiled[:, : 2 * span * span].reshape(groups, span, 2 * span)


def windows(extended, span):
    count = (extended.shape[0] - span) // span
    first = extended[:-span].reshape(count, span, extended.shape[1])
    second = extended[span:].reshape(count, span, extended.shape[1])
    return jnp.concatenate([first, second], axis=1)


def convolve(matrix, extended, span, group):
    blocks = windows(extended, span)
    count, _, width = blocks.shape
    split = blocks.reshape(count, 2 * span, width // group, group)
    result = jnp.einsum("gts,bsgc->btgc", matrix, split, precision=lax.Precision.HIGHEST)
    return result.reshape(count * span, width)


def shards(query_in, key_in, value_in, filters, out_weight, out_grad):
    f32 = jnp.float32
    bf16 = jnp.bfloat16
    tokens, width = query_in.shape
    span = filters.shape[1]
    group = width // filters.shape[0]
    total_tokens = tokens * lax.axis_size("row")
    key32 = key_in.astype(f32)
    value32 = value_in.astype(f32)
    query32 = query_in.astype(f32)
    product = key32 * value32
    key_rim, value_rim = from_behind((key_in[-span:], value_in[-span:]), "row", 1)
    product_rim = key_rim.astype(f32) * value_rim.astype(f32)
    product_ext = jnp.concatenate([product_rim, product], 0)
    conv = convolve(toeplitz(filters, True), product_ext, span, group)
    gated = (query32 * conv).astype(bf16)
    panel = lax.all_gather(gated, "col", axis=1, tiled=True)
    weights = lax.all_gather(out_weight, "row", axis=0, tiled=True)
    mixed_sum = jnp.dot(panel, weights, preferred_element_type=f32)
    partial_value = lax.dot_general(
        out_grad, weights, (((1,), (1,)), ((), ())), preferred_element_type=f32
    )
    mixed = mixed_sum.astype(bf16)
    grad_gated = lax.psum_scatter(
        partial_value.astype(jnp.bfloat16), "col", scatter_dimension=1, tiled=True
    ).astype(jnp.float32)
    query_grad = (grad_gated * conv).astype(bf16)
    grad_conv = grad_gated * query32
    grad_rim = from_behind(grad_conv[:span].astype(jnp.bfloat16), "row", -1).astype(jnp.float32)
    grad_ext = jnp.concatenate([grad_conv, grad_rim], 0)
    grad_product = convolve(toeplitz(filters, False), grad_ext, span, group)
    key_grad = (grad_product * value32).astype(bf16)
    value_grad = (grad_product * key32).astype(bf16)
    count = tokens // span
    groups = width // group
    grad_blocks = grad_conv.reshape(count, span, groups, group)
    product_blocks = windows(product_ext, span).reshape(count, 2 * span, groups, group)
    corr = jnp.einsum(
        "btgc,bsgc->gts", grad_blocks, product_blocks, precision=lax.Precision.HIGHEST
    )
    flat = jnp.concatenate(
        [corr.reshape(groups, 2 * span * span), jnp.zeros((groups, span), f32)], 1
    )
    skewed = flat.reshape(groups, span, 2 * span + 1)[:, :, 1 : span + 1]
    local_taps = jnp.sum(skewed, axis=1)[:, ::-1]
    filter_grad = lax.psum(local_taps, "row") * (1.0 / math.sqrt(total_tokens * group))
    weight_sum = lax.psum_scatter(
        lax.dot_general(
            panel, out_grad, (((0,), (0,)), ((), ())), preferred_element_type=f32
        ).astype(jnp.bfloat16),
        "row",
        scatter_dimension=0,
        tiled=True,
    ).astype(jnp.float32)
    weight_grad = (weight_sum * (1.0 / math.sqrt(total_tokens))).astype(bf16)
    return (mixed, query_grad, key_grad, value_grad, weight_grad, filter_grad)


def solution(mesh):
    placed = (
        P("row", "col"),
        P("row", "col"),
        P("row", "col"),
        P("col", None),
        P("row", "col"),
        P("row", "col"),
    )
    return jax.shard_map(
        shards,
        mesh=mesh,
        in_specs=placed,
        out_specs=(
            P("row", "col"),
            P("row", "col"),
            P("row", "col"),
            P("row", "col"),
            P("row", "col"),
            P("col", None),
        ),
        check_vma=False,
    )
```

profile of v0, /device:TPU:0, one launch (start us, length us, event | category | flops | bytes accessed | tf_op | source)
XLA Modules:
  0.0 819.3 jit_solution(8561546473304693908)
XLA Ops:
  8.0 165.5 %all-gather.5.cloned.1.call-done = bf16[8192,2048]{1,0:T(8,128)(2,1)} async-done(((bf16[1024,2048]{1,0:T(8,128)(2,1)}), bf16[8192,2048]{1,0:T(8,128)(2,1)}) %all-gather.5.cloned.1.call-update) | async-done | bytes 33554448 | tf_op jit(solution)/shard_map/all_gather | solution.py:64
  173.4 16.7 %convolution_convert_fusion.1 = bf16[256,8192]{1,0:T(8,128)(2,1)} fusion(bf16[256,2048]{1,0:T(8,128)(2,1)S(1)} %copy-done, bf16[8192,2048]{1,0:T(8,128)(2,1)} %all-gather.5.cloned.1.call-done), kind=kOutput, calls=%fused_computation.1 | convolution fusion | flops 8592031744 | bytes 38797312 | tf_op jit(solution)/shard_map/dot_general | solution.py:66
  192.8 3.0 collective-permute-start
  198.4 3.2 collective-permute-start.1
  201.8 65.3 %reduce-scatter.3.cloned.1.call-done = bf16[256,2048]{1,0:T(8,128)(2,1)} async-done(((bf16[256,8192]{1,0:T(8,128)(2,1)}), bf16[256,2048]{1,0:T(8,128)(2,1)}) %reduce-scatter.3.cloned.1.call-update) | async-done | bytes 1048592 | tf_op jit(solution)/shard_map/reduce_scatter | solution.py:70
  271.4 7.0 tile.20
  278.4 18.0 %tile.21 = f32[128,32896]{0,1:T(8,128)} reshape(f32[128,128,257]{0,2,1:T(8,128)} %tile.20) | data formatting | bytes 33685504 | tf_op jit(solution)/shard_map/tile | solution.py:28
  296.4 11.3 %slice.38 = f32[128,32768]{0,1:T(8,128)} slice(f32[128,32896]{0,1:T(8,128)} %tile.21), slice={[0:128], [0:32768]} | slice | bytes 33554432 | tf_op jit(solution)/shard_map/slice | solution.py:29
  307.7 17.7 %copy.61 = f32[128,128,256,1]{2,1,3,0:T(8,128)} copy(f32[128,128,256,1]{0,2,1,3:T(8,128)} %bitcast.54) | data formatting | bytes 33554432 | tf_op jit(solution)/shard_map/reshape | solution.py:29
  325.5 7.1 tile.8
  332.5 17.6 %tile.9 = f32[128,32896]{0,1:T(8,128)} reshape(f32[128,128,257]{0,2,1:T(8,128)} %tile.8) | data formatting | bytes 33685504 | tf_op jit(solution)/shard_map/tile | solution.py:28
  350.1 11.4 %slice.36 = f32[128,32768]{0,1:T(8,128)} slice(f32[128,32896]{0,1:T(8,128)} %tile.9), slice={[0:128], [0:32768]} | slice | bytes 33554432 | tf_op jit(solution)/shard_map/slice | solution.py:29
  361.4 17.7 %copy.60 = f32[128,128,256,1]{2,1,3,0:T(8,128)} copy(f32[128,128,256,1]{0,2,1,3:T(8,128)} %bitcast.55) | data formatting | bytes 33554432 | tf_op jit(solution)/shard_map/reshape | solution.py:29
  379.1 2.3 convert_multiply_fusion.6
  383.2 3.3 concatenate.37
  386.5 3.1 copy.50
  398.4 19.9 %fusion.8 = f32[2,128,128,16]{1,3,0,2:T(8,128)S(1)} fusion(f32[128,128,256,1]{2,1,3,0:T(8,128)} %copy.61, f32[2,128,128,16]{1,3,0,2:T(8,128)S(1)} %copy.51, f32[2,128,128,16]{1,3,0,2:T(8,128)S(1)} %copy-done.4), kind=kOutput, calls=%fused_computation.25 | convolution fusion | flops 1611661312 | bytes 23068672 | tf_op jit(solution)/shard_map/gts,bsgc->btgc/dot_general | solution.py:43
  424.0 2.7 pad_maximum_fusion.1
  426.6 3.4 concatenate.33
  432.3 21.5 %convolution_bitcast_fusion.1 = f32[2,128,128,16]{1,3,0,2:T(8,128)S(1)} fusion(f32[2,256,128,16]{1,3,0,2:T(8,128)S(1)} %copy_dynamic-update-slice_fusion, f32[128,128,256,1]{2,1,3,0:T(8,128)} %copy.60), kind=kOutput, calls=%fused_computation.26 | convolution fusion | flops 1610612736 | bytes 23068672 | tf_op jit(solution)/shard_map/gts,bsgc->btgc/dot_general | solution.py:43
  456.8 4.3 fusion.7
  461.1 18.0 %convolution_bitcast_fusion = f32[128,128,256]{2,1,0:T(8,128)} fusion(f32[2,256,128,16]{1,3,0,2:T(8,128)} %copy-done.1, f32[2,128,128,16]{1,0,3,2:T(2,128)S(1)} %copy-done.2), kind=kOutput, calls=%fused_computation.2 | convolution fusion | flops 1610612736 | bytes 23068672 | tf_op jit(solution)/shard_map/btgc,bsgc->gts/dot_general | solution.py:84
  479.1 17.9 %copy.69 = f32[128,128,256]{0,2,1:T(8,128)} copy(f32[128,128,256]{2,1,0:T(8,128)} %convolution_bitcast_fusion) | data formatting | bytes 33554432 | tf_op jit(solution)/shard_map/reshape | solution.py:88
  497.0 13.5 %concatenate.42 = f32[128,32896]{0,1:T(8,128)} pad(f32[128,32768]{0,1:T(8,128)} %bitcast.53, f32[]{:T(128)} %constant.3.clone.1), padding=0_0x0_128 | pad | bytes 33619972 | tf_op jit(solution)/shard_map/concatenate | solution.py:87
  510.5 17.6 %reshape.61 = f32[128,128,257]{0,2,1:T(8,128)} reshape(f32[128,32896]{0,1:T(8,128)} %concatenate.42) | data formatting | bytes 33685504 | tf_op jit(solution)/shard_map/reshape | solution.py:90
  528.1 4.4 slice_reduce_fusion
  533.3 10.8 %all-gather.3.cloned.1.call-done = bf16[256,8192]{1,0:T(8,128)(2,1)} async-done(((bf16[256,2048]{1,0:T(8,128)(2,1)}), bf16[256,8192]{1,0:T(8,128)(2,1)}) %all-gather.3.cloned.1.call-update) | async-done | bytes 4194320 | tf_op jit(solution)/shard_map/all_gather | solution.py:63
  544.1 16.5 %convolution_convert_fusion = bf16[8192,2048]{1,0:T(8,128)(2,1)} fusion(bf16[256,8192]{1,0:T(8,128)(2,1)} %all-gather.3.cloned.1.call-done, bf16[256,2048]{1,0:T(8,128)(2,1)S(1)} %copy-done), kind=kOutput, calls=%fused_computation | convolution fusion | flops 8606711808 | bytes 38797312 | tf_op jit(solution)/shard_map/dot_general | solution.py:94
  564.6 34.3 %all-reduce.4.cloned.1.call-done = f32[128,128]{0,1:T(8,128)} async-done(((f32[128,128]{0,1:T(8,128)}), f32[128,128]{0,1:T(8,128)}) %all-reduce.4.cloned.1.call-update) | async-done | bytes 65552 | tf_op jit(solution)/shard_map/psum | solution.py:92
  600.4 20.2 %convolution_convert_fusion.2 = bf16[256,2048]{1,0:T(8,128)(2,1)} fusion(bf16[256,8192]{1,0:T(8,128)(2,1)} %all-gather.3.cloned.1.call-done, bf16[8192,2048]{1,0:T(8,128)(2,1)} %all-gather.5.cloned.1.call-done), kind=kOutput, calls=%fused_computation.15 | convolution fusion | flops 8590458880 | bytes 38797312 | tf_op jit(solution)/shard_map/dot_general | solution.py:65
  620.7 186.3 %reduce-scatter.5.cloned.1.call-done = bf16[1024,2048]{1,0:T(8,128)(2,1)} async-done(((bf16[8192,2048]{1,0:T(8,128)(2,1)}), bf16[1024,2048]{1,0:T(8,128)(2,1)}) %reduce-scatter.5.cloned.1.call-update) | async-done | bytes 4194320 | tf_op jit(solution)/shard_map/reduce_scatter | solution.py:93
  806.9 5.6 multiply_convert_fusion
  (73 shorter events, 38.3 us)
Async XLA Ops:
  7.2 166.3 %copy-start = (bf16[256,2048]{1,0:T(8,128)(2,1)S(1)}, bf16[256,2048]{1,0:T(8,128)(2,1)}, u32[]{:S(2)}) copy-start(bf16[256,2048]{1,0:T(8,128)(2,1)} %param.11) | copy-start | bytes 3145732
  7.2 166.2 %all-gather.5.cloned.1.call-start = ((), (), s32[]{:S(2)}) async-start(), calls=%async_computation.3 | async-start | bytes 37748736 | tf_op jit(solution)/shard_map/all_gather | solution.py:64
  7.9 259.2 %reduce-scatter.3.cloned.1.call-start = ((), (), s32[]{:S(2)}) async-start(), calls=%async_computation.4 | async-start | bytes 5242880 | tf_op jit(solution)/shard_map/reduce_scatter | solution.py:70
  190.1 1.2 copy-start.11
  190.2 11.4 %copy-start.12 = (f32[128,128]{1,0:T(8,128)S(1)}, f32[128,128]{1,0:T(8,128)}, u32[]{:S(2)}) copy-start(f32[128,128]{1,0:T(8,128)} %param.9) | copy-start | bytes 196612
  190.2 353.9 %all-gather.3.cloned.1.call-start = ((), (), s32[]{:S(2)}) async-start(), calls=%async_computation.2 | async-start | bytes 5242880 | tf_op jit(solution)/shard_map/all_gather | solution.py:63
  191.9 9.9 %copy-start.5 = (bf16[256,2048]{0,1:T(8,128)(2,1)}, bf16[256,2048]{0,1:T(8,128)(2,1)S(1)}, u32[]{:S(2)}) copy-start(bf16[256,2048]{0,1:T(8,128)(2,1)S(1)} %copy.37) | copy-start | bytes 3145732
  192.8 186.3 %collective-permute-start = (bf16[128,2048]{0,1:T(8,128)(2,1)}, bf16[128,2048]{0,1:T(8,128)(2,1)}, u32[]{:S(2)}, u32[]{:S(2)}) collective-permute-start(bf16[128,2048]{0,1:T(8,128)(2,1)} %slice.34), channel_id=1, source_target_pairs={{0,4},{4,8},{8,12},{12,16},{16,20},{20,24},{24,28},{1,5},{5,9},{9,... | collective-permute-start | bytes 1572872 | tf_op jit(solution)/shard_map/ppermute | solution.py:12
  197.5 4.3 copy-start.7
  198.4 180.8 %collective-permute-start.1 = (bf16[128,2048]{0,1:T(8,128)(2,1)}, bf16[128,2048]{0,1:T(8,128)(2,1)}, u32[]{:S(2)}, u32[]{:S(2)}) collective-permute-start(bf16[128,2048]{0,1:T(8,128)(2,1)} %slice.35), channel_id=1, source_target_pairs={{0,4},{4,8},{8,12},{12,16},{16,20},{20,24},{24,28},{1,5},{5,9},{9,... | collective-permute-start | bytes 1572872 | tf_op jit(solution)/shard_map/ppermute | solution.py:12
  269.8 119.7 %collective-permute-start.2 = (bf16[128,2048]{1,0:T(8,128)(2,1)}, bf16[128,2048]{1,0:T(8,128)(2,1)}, u32[]{:S(2)}, u32[]{:S(2)}) collective-permute-start(bf16[128,2048]{1,0:T(8,128)(2,1)} %slice.42), channel_id=1, source_target_pairs={{4,0},{8,4},{12,8},{16,12},{20,16},{24,20},{28,24},{5,1},{9,5},{13... | collective-permute-start | bytes 1572872 | tf_op jit(solution)/shard_map/ppermute | solution.py:12
  396.2 2.2 copy-start.4
  418.3 1.2 copy-start.6
  418.3 1.5 copy-start.8
  426.6 5.3 copy-start.3
  432.2 21.5 %copy-start.1 = (f32[2,256,128,16]{1,3,0,2:T(8,128)}, f32[2,256,128,16]{1,3,0,2:T(8,128)S(1)}, u32[]{:S(2)}) copy-start(f32[2,256,128,16]{1,3,0,2:T(8,128)S(1)} %copy_dynamic-update-slice_fusion) | copy-start | bytes 12582916
  456.8 4.3 copy-start.2
  461.1 137.8 %all-reduce.4.cloned.1.call-start = ((), (), s32[]{:S(2)}) async-start(), calls=%async_computation.6 | async-start | bytes 131072 | tf_op jit(solution)/shard_map/psum | solution.py:92
  533.3 273.7 %reduce-scatter.5.cloned.1.call-start = ((), (), s32[]{:S(2)}) async-start(), calls=%async_computation.5 | async-start | bytes 37748736 | tf_op jit(solution)/shard_map/reduce_scatter | solution.py:93
  560.5 1.2 copy-start.10
  560.5 2.6 copy-start.9
Sparse Core Ops, SparseCore 0:
  9.9 163.4 all-gather.4
  190.3 76.7 reduce-scatter.2
  461.2 82.8 all-gather.2
  547.8 50.9 all-reduce.3
  602.3 204.6 reduce-scatter.4
where the time goes:
time: 826 us; the launch traced here: 819 us
  waiting for transfers between devices  463 us (56%)
  local copies, waits for them, and re-layouts  195 us (24%)
  matrix products  113 us (14%)
  other arithmetic  26.6 us (3%)
  between operations  14.3 us (2%)
    reduce_scatter x1, waiting for transfers between devices, shards(): lax.psum_scatter(lax.dot_general(panel, out_grad, (((0,), (0,)), ((), ())...  186 us
    all_gather x1, waiting for transfers between devices, shards(): weights = lax.all_gather(out_weight, 'row', axis=0, tiled=True)  165 us
    reduce_scatter x1, waiting for transfers between devices, shards(): lax.psum_scatter(partial_value.astype(jnp.bfloat16), 'col', scatter_dimen...  65.3 us
    another operation x4, local copies, waits for them, and re-layouts, toeplitz(): tiled = jnp.tile(template, (1, span))  49.7 us
    dot_general x2, matrix products, convolve(): jnp.einsum('gts,bsgc->btgc', matrix, split, precision=lax.Precision.HIGHEST)  41.4 us
    reshape x2, local copies, waits for them, and re-layouts, toeplitz(): return tiled[:, :2 * span * span].reshape(groups, span, 2 * span)  35.4 us
    psum x1, waiting for transfers between devices, shards(): lax.psum(local_taps, 'row') * (1.0 / math.sqrt(total_tokens * group))  34.3 us
    slice x2, local copies, waits for them, and re-layouts, toeplitz(): return tiled[:, :2 * span * span].reshape(groups, span, 2 * span)  22.6 us
  transfers between devices with their start and end apart: 8, of which 5 were waited for; matrix products, arithmetic and copies ran while one was open for 29% of the time, Pallas kernels for 0%

commit v1 on v0

v1 whole, which is shorter than its diff:
```python
import functools
import math

import jax
import jax.numpy as jnp
from jax import lax
from jax.experimental import pallas as pl
from jax.experimental.pallas import tpu as pltpu
from jax.sharding import PartitionSpec as P

LANES = 128
STEP = 512
f32 = jnp.float32
bf16 = jnp.bfloat16


def band(base, index, span):
    row = jnp.broadcast_to(base[index : index + 1], (span, 2 * span))
    return pltpu.roll(row, 0, 1, stride=1, stride_axis=0).astype(bf16)


def banded(base, column, first, owner, span, group):
    total = jnp.zeros(owner.shape, f32)
    for g in range(LANES // group):
        value = jnp.dot(band(base, first + g, span), column, preferred_element_type=f32)
        total = jnp.where(owner == g, value, total)
    return total


def conv_kernel(span, group, turn_ref, base_ref, before_ref, here_ref, query_ref, gated_ref, conv_ref):
    window = jnp.concatenate([before_ref[...], here_ref[...]], 0)
    owner = lax.broadcasted_iota(jnp.int32, (span, LANES), 1) // group
    for start in range(0, window.shape[1], LANES):
        cut = slice(start, start + LANES)
        conv = banded(base_ref[...], window[:, cut], start // group, owner, span, group)
        conv_ref[:, cut] = conv
        gated_ref[:, cut] = (query_ref[:, cut].astype(f32) * conv).astype(bf16)


def conv_call(turn, base, before, before_at, here, at, query, span, group):
    width = here.shape[1]
    lanes = min(width, STEP)

    def block(row):
        return pl.BlockSpec((span, lanes), lambda i, turn: (row, i))

    return pl.pallas_call(
        functools.partial(conv_kernel, span, group),
        grid_spec=pltpu.PrefetchScalarGridSpec(
            num_scalar_prefetch=1,
            grid=(width // lanes,),
            in_specs=[
                pl.BlockSpec((lanes // group, 2 * span), lambda i, turn: (i, 0)),
                block(before_at),
                block(at),
                block(at),
            ],
            out_specs=[
                pl.BlockSpec((span, lanes), lambda i, turn: (0, i ^ turn[0])),
                block(0),
            ],
        ),
        out_shape=[
            jax.ShapeDtypeStruct((span, width), bf16),
            jax.ShapeDtypeStruct((span, width), f32),
        ],
        cost_estimate=pl.CostEstimate(
            flops=4 * span * span * width * LANES // group,
            bytes_accessed=12 * span * width,
            transcendentals=0,
        ),
        name="conv",
    )(turn, base, before, here, query)


def taps_kernel(span, group, turn_ref, grad_ref, low_ref, high_ref, query_ref, rim_ref, product_ref, query_grad_ref, grad_conv_ref, taps_ref):
    rows = lax.broadcasted_iota(jnp.int32, (span, span), 0)
    columns = lax.broadcasted_iota(jnp.int32, (span, span), 1)
    flip = jnp.where(rows + columns == span - 1, 1.0, 0.0).astype(bf16)
    owner = lax.broadcasted_iota(jnp.int32, (span, 2 * LANES), 1) % LANES // group
    for start in range(0, query_ref.shape[1], LANES):
        cut = slice(start, start + LANES)
        grad = grad_ref[0, :, cut].astype(f32)
        conv = jnp.concatenate([low_ref[:, cut], high_ref[:, cut]], 0)
        query_grad_ref[:, cut] = (grad * conv).astype(bf16)
        grad_conv = (grad * query_ref[:, cut].astype(f32)).astype(bf16)
        grad_conv_ref[:, cut] = grad_conv
        left = jnp.concatenate([grad_conv[:span], grad_conv[span:]], 1)
        left = jnp.dot(flip, left, preferred_element_type=f32).astype(bf16)
        late = product_ref[:, cut]
        early = jnp.concatenate([rim_ref[:, cut], late[:span]], 0)
        right = jnp.concatenate([early, late], 1)
        for g in range(LANES // group):
            one = jnp.where(owner == g, left, jnp.zeros_like(left))
            corr = lax.dot_general(one, right, (((1,), (1,)), ((), ())), preferred_element_type=f32)
            lined = pltpu.roll(corr, 0, 1, stride=1, stride_axis=0)
            at = start // group + g
            taps_ref[at : at + 1] = jnp.sum(lined[:, span:], axis=0, keepdims=True)


def taps_call(turn, grad, low, high, query, rim, product, span, group):
    tokens, width = query.shape
    lanes = grad.shape[2]

    def block(rows):
        return pl.BlockSpec((rows, lanes), lambda i, turn: (0, i))

    return pl.pallas_call(
        functools.partial(taps_kernel, span, group),
        grid_spec=pltpu.PrefetchScalarGridSpec(
            num_scalar_prefetch=1,
            grid=(width // lanes,),
            in_specs=[
                pl.BlockSpec((1, tokens, lanes), lambda i, turn: (i ^ turn[0], 0, 0)),
                block(span),
                block(span),
                block(tokens),
                block(span),
                block(tokens),
            ],
            out_specs=[
                block(tokens),
                block(tokens),
                pl.BlockSpec((lanes // group, span), lambda i, turn: (i, 0)),
            ],
        ),
        out_shape=[
            jax.ShapeDtypeStruct((tokens, width), bf16),
            jax.ShapeDtypeStruct((tokens, width), bf16),
            jax.ShapeDtypeStruct((width // group, span), f32),
        ],
        cost_estimate=pl.CostEstimate(
            flops=8 * span * tokens * width * LANES // group,
            bytes_accessed=16 * tokens * width,
            transcendentals=0,
        ),
        name="taps",
    )(turn, grad, low, high, query, rim, product)


def back_kernel(span, group, base_ref, grad_conv_ref, rim_ref, key_ref, value_ref, key_grad_ref, value_grad_ref):
    owner = lax.broadcasted_iota(jnp.int32, (span, 2 * LANES), 1) % LANES // group
    for start in range(0, key_ref.shape[1], LANES):
        cut = slice(start, start + LANES)
        here = grad_conv_ref[:, cut]
        after = jnp.concatenate([here[span:], rim_ref[:, cut]], 0)
        column = jnp.concatenate([here, after], 1)
        total = banded(base_ref[...], column, start // group, owner, span, group)
        product = jnp.concatenate([total[:, :LANES], total[:, LANES:]], 0)
        key_grad_ref[:, cut] = (product * value_ref[:, cut].astype(f32)).astype(bf16)
        value_grad_ref[:, cut] = (product * key_ref[:, cut].astype(f32)).astype(bf16)


def back_call(base, grad_conv, rim, key, value, span, group):
    tokens, width = key.shape
    lanes = min(width, STEP)

    def block(rows):
        return pl.BlockSpec((rows, lanes), lambda i: (0, i))

    return pl.pallas_call(
        functools.partial(back_kernel, span, group),
        grid=(width // lanes,),
        in_specs=[
            pl.BlockSpec((lanes // group, 2 * span), lambda i: (i, 0)),
            block(tokens),
            block(span),
            block(tokens),
            block(tokens),
        ],
        out_specs=[block(tokens), block(tokens)],
        out_shape=[
            jax.ShapeDtypeStruct((tokens, width), bf16),
            jax.ShapeDtypeStruct((tokens, width), bf16),
        ],
        cost_estimate=pl.CostEstimate(
            flops=4 * span * tokens * width * LANES // group,
            bytes_accessed=12 * tokens * width,
            transcendentals=0,
        ),
        name="back",
    )(base, grad_conv, rim, key, value)


def from_behind(shard, by):
    size = lax.axis_size("row")
    pairs = [(i, i + by) for i in range(size) if 0 <= i + by < size]
    return lax.ppermute(shard, "row", pairs)


def exchange(shard, bits):
    size = lax.axis_size("row")
    return lax.ppermute(shard, "row", [(i, i ^ bits) for i in range(size)])


def ring(shard):
    size = lax.axis_size("col")
    return lax.ppermute(shard, "col", [(i, (i + 1) % size) for i in range(size)])


def dot_nt(a, b):
    return lax.dot_general(a, b, (((1,), (1,)), ((), ())), preferred_element_type=f32)


def dot_tn(a, b):
    return lax.dot_general(a, b, (((0,), (0,)), ((), ())), preferred_element_type=f32)


def projection(gated, out_weight, out_grad, total_tokens):
    cols = lax.axis_size("col")
    core = lax.axis_index("row") % 2
    chip = lax.axis_index("row") // 2
    plane = lax.axis_index("col")
    span, width = gated[0].shape
    blocks = len(gated)
    half = out_weight.shape[0]
    lanes = width // cols
    pair = jnp.concatenate([out_weight, exchange(out_weight, 1)], 0)

    sent = [out_grad] + [exchange(out_grad, 2 * d) for d in range(1, cols)]
    grads = jnp.concatenate([g[h * span : (h + 1) * span] for h in range(blocks) for g in sent], 0)

    total = None
    for step in range(cols):
        part = (plane + 2 * cols - 1 - step) % cols
        rows = lax.dynamic_slice_in_dim(pair, part * lanes, lanes, 0)
        value = dot_nt(grads, rows)
        if total is not None:
            value = value + ring(total).astype(f32)
        total = value.astype(bf16)
    summed = total.reshape(blocks, cols, span, lanes)
    grad_gated = []
    for e in range(cols):
        piece = lax.dynamic_index_in_dim(summed, chip ^ plane ^ e, 1, False)
        pairs = [
            ((2 * q + s) * cols + j, (2 * (j ^ e) + s) * cols + q)
            for q in range(cols)
            for s in range(2)
            for j in range(cols)
        ]
        grad_gated.append(lax.ppermute(piece.reshape(blocks * span, lanes), ("row", "col"), pairs))
    grad_gated = jnp.stack(grad_gated)

    held = [None] * blocks
    mixed = [None] * blocks
    for h in reversed(range(blocks)):
        pieces = [gated[h]]
        for _ in range(1, cols):
            pieces.append(ring(pieces[-1]))
        stack = jnp.stack(pieces)
        own = lax.dynamic_index_in_dim(stack, (plane - chip) % cols, 0, False)
        came = []
        for d in range(1, cols):
            piece = lax.dynamic_index_in_dim(stack, (plane - (chip ^ d)) % cols, 0, False)
            came.append(exchange(piece, 2 * d))
        held[h] = [own] + came
        partial = jnp.dot(jnp.concatenate(came, 0), pair, preferred_element_type=f32).astype(bf16)
        value = jnp.dot(own, pair, preferred_element_type=f32)
        for d in range(1, cols):
            value = value + exchange(partial[(d - 1) * span : d * span], 2 * d).astype(f32)
        mixed[h] = value.astype(bf16)
    mixed = jnp.concatenate(mixed, 0)

    tokens = jnp.concatenate([piece for h in held for piece in h], 0)
    other = exchange(dot_tn(tokens[:, half:], grads).astype(bf16), 1)
    weight_sum = dot_tn(tokens[:, :half], grads) + other.astype(f32)
    weight_grad = (weight_sum * (1.0 / math.sqrt(total_tokens))).astype(bf16)
    return mixed, grad_gated, weight_grad


def projection_gathered(gated, out_weight, out_grad, total_tokens):
    panel = lax.all_gather(jnp.concatenate(gated, 0), "col", axis=1, tiled=True)
    weights = lax.all_gather(out_weight, "row", axis=0, tiled=True)
    mixed = jnp.dot(panel, weights, preferred_element_type=f32).astype(bf16)
    partial = dot_nt(out_grad, weights).astype(bf16)
    grad_gated = lax.psum_scatter(partial, "col", scatter_dimension=1, tiled=True)
    tokens, width = grad_gated.shape
    lanes = min(width, STEP)
    grad_gated = grad_gated.reshape(tokens, width // lanes, lanes).transpose(1, 0, 2)
    weight_sum = lax.psum_scatter(
        dot_tn(panel, out_grad).astype(bf16), "row", scatter_dimension=0, tiled=True
    ).astype(f32)
    weight_grad = (weight_sum * (1.0 / math.sqrt(total_tokens))).astype(bf16)
    return mixed, grad_gated, weight_grad


def shards(query_in, key_in, value_in, filters, out_weight, out_grad):
    tokens, width = query_in.shape
    groups, span = filters.shape
    group = width // groups
    rows, cols = lax.axis_size("row"), lax.axis_size("col")
    total_tokens = tokens * rows
    even = cols & (cols - 1) == 0
    paired = even and rows == 2 * cols and width == 2 * out_weight.shape[0] and width == cols * STEP
    core = lax.axis_index("row") % 2
    chip = lax.axis_index("row") // 2
    turn_gated = core * (cols // 2) if paired else core * 0
    turn_grad = turn_gated ^ chip if paired else core * 0

    product = (key_in.astype(f32) * value_in.astype(f32)).astype(bf16)
    rim = from_behind(product[-span:], 1)
    zeros = jnp.zeros((groups, span - 1), f32)
    causal = jnp.concatenate([zeros[:, :1], filters[:, ::-1], zeros], 1)
    anticausal = jnp.concatenate([filters, zeros, zeros[:, :1]], 1)
    turn = turn_gated.astype(jnp.int32).reshape(1)
    gated_high, conv_high = conv_call(turn, causal, product, 0, product, 1, query_in, span, group)
    gated_low, conv_low = conv_call(turn, causal, rim, 0, product, 0, query_in, span, group)

    project = projection if paired else projection_gathered
    mixed, grad_gated, weight_grad = project([gated_low, gated_high], out_weight, out_grad, total_tokens)

    turn = turn_grad.astype(jnp.int32).reshape(1)
    query_grad, grad_conv, taps = taps_call(turn, grad_gated, conv_low, conv_high, query_in, rim, product, span, group)
    grad_rim = from_behind(grad_conv[:span], -1)
    key_grad, value_grad = back_call(anticausal, grad_conv, grad_rim, key_in, value_in, span, group)
    bits = 1
    while bits < rows:
        taps = taps + exchange(taps, bits)
        bits *= 2
    filter_grad = taps[:, ::-1] * (1.0 / math.sqrt(total_tokens * group))
    return (mixed, query_grad, key_grad, value_grad, weight_grad, filter_grad)


def solution(mesh):
    placed = (
        P("row", "col"),
        P("row", "col"),
        P("row", "col"),
        P("col", None),
        P("row", "col"),
        P("row", "col"),
    )
    return jax.shard_map(
        shards,
        mesh=mesh,
        in_specs=placed,
        out_specs=(
            P("row", "col"),
            P("row", "col"),
            P("row", "col"),
            P("row", "col"),
            P("row", "col"),
            P("col", None),
        ),
        check_vma=False,
    )
```

time: 826 us -> 337 us (0.41)
  waiting for transfers between devices: 463 us -> 187 us
  local copies, waits for them, and re-layouts: 195 us -> 21.8 us
  matrix products: 113 us -> 37.8 us
  starting transfers between devices: 7.65 us -> 53.6 us
  Pallas kernels: 0 us -> 27.7 us
  other arithmetic: 26.6 us -> 7.27 us
  between operations: 14.3 us -> 1.11 us
    reduce_scatter x2 -> x0, waiting for transfers between devices: 252 us -> none  [the longest x1 186 us: shards(): lax.psum_scatter(lax.dot_general(panel, out_grad, (((0,), (0,)), ((), ())...]
    ppermute x3 -> x35, waiting for transfers between devices: 0.01 us -> 187 us  [the longest x9 92.9 us: ring(): lax.ppermute(shard, 'col', [(i, (i + 1) % size) for i in range(size)])]
    all_gather x2 -> x0, waiting for transfers between devices: 176 us -> none  [the longest x1 165 us: shards(): weights = lax.all_gather(out_weight, 'row', axis=0, tiled=True)]
    dot_general x6 -> x10, matrix products: 113 us -> 37.8 us  [the longest x2 14.5 us: dot_tn(): lax.dot_general(a, b, (((0,), (0,)), ((), ())), preferred_element_type=f32)]
    reshape x5 -> x0, local copies, waits for them, and re-layouts: 72.7 us -> none  [the longest x2 35.4 us: toeplitz(): return tiled[:, :2 * span * span].reshape(groups, span, 2 * span)]
    another operation x5 -> x1, local copies, waits for them, and re-layouts: 49.7 us -> 0.01 us  [the longest x4 49.7 us: toeplitz(): tiled = jnp.tile(template, (1, span))]
    ppermute x3 -> x35, starting transfers between devices: 7.45 us -> 53.6 us  [the longest x20 38.7 us: exchange(): return lax.ppermute(shard, 'row', [(i, i ^ bits) for i in range(size)])]
    psum x1 -> x0, waiting for transfers between devices: 34.3 us -> none  [shards(): lax.psum(local_taps, 'row') * (1.0 / math.sqrt(total_tokens * group))]
  transfers between devices with their start and end apart: 8 -> 35, of which waited for: 5 -> 18; matrix products, arithmetic and copies ran while one was open for 29% -> 18% of each run, Pallas kernels for 0% -> 6%
where the time goes in v1:
time: 337 us
  waiting for transfers between devices  187 us (55%)
  starting transfers between devices  53.6 us (16%)
  matrix products  37.8 us (11%)
  Pallas kernels  27.7 us (8%)
  local copies, waits for them, and re-layouts  21.8 us (6%)
  other arithmetic  7.27 us (2%)
    ppermute x9, waiting for transfers between devices, ring(): lax.ppermute(shard, 'col', [(i, (i + 1) % size) for i in range(size)])  92.9 us
    ppermute x20, waiting for transfers between devices, exchange(): return lax.ppermute(shard, 'row', [(i, i ^ bits) for i in range(size)])  58.4 us
    ppermute x20, starting transfers between devices, exchange(): return lax.ppermute(shard, 'row', [(i, i ^ bits) for i in range(size)])  38.7 us
    ppermute x4, waiting for transfers between devices, projection(): lax.ppermute(piece.reshape(blocks * span, lanes), ('row', 'col'), pairs)  36.1 us
    unnamed x45, local copies, waits for them, and re-layouts  16.5 us
    dot_general x2, matrix products, dot_tn(): lax.dot_general(a, b, (((0,), (0,)), ((), ())), preferred_element_type=f32)  14.5 us
    pallas_call x2, Pallas kernels, conv_call(): pl.pallas_call(functools.partial(conv_kernel, span, group), grid_spec=plt...  11 us
    pallas_call x1, Pallas kernels, taps_call(): pl.pallas_call(functools.partial(taps_kernel, span, group), grid_spec=plt...  10.1 us
  transfers between devices with their start and end apart: 35, of which 18 were waited for; matrix products, arithmetic and copies ran while one was open for 18% of the time, Pallas kernels for 6%

profile of v1, /device:TPU:0, one launch (start us, length us, event | category | flops | bytes accessed | tf_op | source)
XLA Modules:
  0.0 336.6 jit_solution(16613093518317962755)
XLA Ops:
  3.6 3.2 collective-permute-start
  11.2 5.5 %conv.3 = (bf16[128,2048]{1,0:T(8,128)(2,1)}, f32[128,2048]{1,0:T(8,128)}) custom-call(s32[1]{0:T(128)} %bitcast.turn_ref, f32[128,256]{1,0:T(8,128)} %get-tuple-element.41.base_ref, bf16[256,2048]{1,0:T(8,128)(2,1)} %copy-done.1, bf16[256,2048]{1,0:T(8,128)(2,1)} %copy-done.1, bf16[256,2048]{1,0:T(8,128)(2,1)} %query_ref.5), custom_call_target="tpu_custom_call" | custom-call | flops 1073741824 | bytes 3145728 | tf_op jit(solution)/shard_map/conv/pallas_call | solution.py:47
  16.7 2.4 collective-permute-start.11
  19.1 5.5 %conv.2 = (bf16[128,2048]{1,0:T(8,128)(2,1)}, f32[128,2048]{1,0:T(8,128)}) custom-call(s32[1]{0:T(128)} %bitcast.turn_ref, f32[128,256]{1,0:T(8,128)} %get-tuple-element.41.base_ref, bf16[128,2048]{1,0:T(8,128)(2,1)} %collective-permute-done.before_ref.rim_ref, bf16[256,2048]{1,0:T(8,128)(2,1)} %copy-done.1, bf16[256,2048]{1,0:T(8,128)(2,1)} %query_ref.5), custom_call_target="tpu_custom_call" | custom-call | flops 1073741824 | bytes 3145728 | tf_op jit(solution)/shard_map/conv/pallas_call | solution.py:47
  27.0 4.8 %constant_dynamic-update-slice_fusion.1 = bf16[2048,2048]{1,0:T(8,128)(2,1)} fusion(bf16[1024,2048]{1,0:T(8,128)(2,1)} %param.10), kind=kLoop, calls=%fused_computation.64 | loop fusion | bytes 8388608
  34.0 10.9 %collective-permute-done.1 = bf16[128,2048]{1,0:T(8,128)(2,1)} collective-permute-done((bf16[128,2048]{1,0:T(8,128)(2,1)}, bf16[128,2048]{1,0:T(8,128)(2,1)}, u32[]{:S(2)}, u32[]{:S(2)}) %collective-permute-start.1) | collective-permute-done | bytes 524320 | tf_op jit(solution)/shard_map/ppermute | solution.py:198
  48.1 12.6 %collective-permute-done.21 = bf16[256,2048]{1,0:T(8,128)(2,1)S(1)} collective-permute-done((bf16[256,2048]{1,0:T(8,128)(2,1)S(1)}, bf16[256,2048]{1,0:T(8,128)(2,1)S(1)}, u32[]{:S(2)}, u32[]{:S(2)}) %collective-permute-start.21) | collective-permute-done | bytes 1048608 | tf_op jit(solution)/shard_map/ppermute | solution.py:193
  66.2 6.6 %collective-permute-done.2 = bf16[128,2048]{1,0:T(8,128)(2,1)S(1)} collective-permute-done((bf16[128,2048]{1,0:T(8,128)(2,1)}, bf16[128,2048]{1,0:T(8,128)(2,1)S(1)}, u32[]{:S(2)}, u32[]{:S(2)}) %collective-permute-start.2) | collective-permute-done | bytes 524320 | tf_op jit(solution)/shard_map/ppermute | solution.py:198
  75.6 18.4 %collective-permute-done.3 = bf16[128,2048]{1,0:T(8,128)(2,1)S(1)} collective-permute-done((bf16[128,2048]{1,0:T(8,128)(2,1)S(1)}, bf16[128,2048]{1,0:T(8,128)(2,1)S(1)}, u32[]{:S(2)}, u32[]{:S(2)}) %collective-permute-start.3) | collective-permute-done | bytes 524320 | tf_op jit(solution)/shard_map/ppermute | solution.py:198
  100.9 9.5 %collective-permute-done.5 = bf16[128,2048]{1,0:T(8,128)(2,1)S(1)} collective-permute-done((bf16[128,2048]{1,0:T(8,128)(2,1)S(1)}, bf16[128,2048]{1,0:T(8,128)(2,1)S(1)}, u32[]{:S(2)}, u32[]{:S(2)}) %collective-permute-start.5) | collective-permute-done | bytes 524320 | tf_op jit(solution)/shard_map/ppermute | solution.py:193
  112.2 22.2 %collective-permute-done.6 = bf16[128,2048]{1,0:T(8,128)(2,1)S(1)} collective-permute-done((bf16[128,2048]{1,0:T(8,128)(2,1)S(1)}, bf16[128,2048]{1,0:T(8,128)(2,1)S(1)}, u32[]{:S(2)}, u32[]{:S(2)}) %collective-permute-start.6) | collective-permute-done | bytes 524320 | tf_op jit(solution)/shard_map/ppermute | solution.py:193
  134.6 9.0 %collective-permute-done.14 = bf16[128,2048]{1,0:T(8,128)(2,1)S(1)} collective-permute-done((bf16[128,2048]{1,0:T(8,128)(2,1)S(1)}, bf16[128,2048]{1,0:T(8,128)(2,1)S(1)}, u32[]{:S(2)}, u32[]{:S(2)}) %collective-permute-start.14) | collective-permute-done | bytes 524320 | tf_op jit(solution)/shard_map/ppermute | solution.py:193
  146.2 2.4 fusion.26
  148.9 6.3 %convolution_convert_fusion = bf16[1024,2048]{1,0:T(8,128)(2,1)} fusion(bf16[1024,2048]{1,0:T(8,128)(2,1)S(1)} %copy-done.8, bf16[1024,2048]{1,0:T(8,128)(2,1)S(1)} %constant_dynamic-update-slice_fusion.2), kind=kOutput, calls=%fused_computation.1 | convolution fusion | flops 4297064448 | bytes 10485760 | tf_op jit(solution)/shard_map/dot_general | solution.py:206
  155.2 18.9 %collective-permute-done.23 = bf16[1024,512]{1,0:T(8,128)(2,1)S(1)} collective-permute-done((bf16[1024,512]{1,0:T(8,128)(2,1)S(1)}, bf16[1024,512]{1,0:T(8,128)(2,1)S(1)}, u32[]{:S(2)}, u32[]{:S(2)}) %collective-permute-start.23) | collective-permute-done | bytes 1048608 | tf_op jit(solution)/shard_map/ppermute | solution.py:198
  174.1 2.4 add_convert_fusion.2
  176.5 3.5 %convolution_convert_fusion.1 = bf16[384,2048]{1,0:T(8,128)(2,1)S(1)} fusion(bf16[2048,2048]{1,0:T(8,128)(2,1)S(1)} %constant_dynamic-update-slice_fusion, bf16[128,2048]{1,0:T(8,128)(2,1)S(1)} %collective-permute-done.16, bf16[128,2048]{1,0:T(8,128)(2,1)S(1)} %collective-permute-done.15, bf16[128,2048]{1,0:T(8,128)(2,1)S(1)} %collective-permute-done.14), kind=kOutput, calls=%fused_computation.2 | convolution fusion | flops 3226730496 | bytes 11534336 | tf_op jit(solution)/shard_map/dot_general | solution.py:257
  183.7 17.2 %collective-permute-done.24 = bf16[1024,512]{1,0:T(8,128)(2,1)S(1)} collective-permute-done((bf16[1024,512]{1,0:T(8,128)(2,1)S(1)}, bf16[1024,512]{1,0:T(8,128)(2,1)S(1)}, u32[]{:S(2)}, u32[]{:S(2)}) %collective-permute-start.24) | collective-permute-done | bytes 1048608 | tf_op jit(solution)/shard_map/ppermute | solution.py:198
  200.8 2.4 add_convert_fusion.1
  203.5 3.5 %convolution_convert_fusion.2 = bf16[384,2048]{1,0:T(8,128)(2,1)S(1)} fusion(bf16[2048,2048]{1,0:T(8,128)(2,1)S(1)} %constant_dynamic-update-slice_fusion, bf16[128,2048]{1,0:T(8,128)(2,1)S(1)} %collective-permute-done.7, bf16[128,2048]{1,0:T(8,128)(2,1)S(1)} %collective-permute-done.6, bf16[128,2048]{1,0:T(8,128)(2,1)S(1)} %collective-permute-done.5), kind=kOutput, calls=%fused_computation.3 | convolution fusion | flops 3226730496 | bytes 11534336 | tf_op jit(solution)/shard_map/dot_general | solution.py:257
  208.2 18.7 %collective-permute-done.25 = bf16[1024,512]{1,0:T(8,128)(2,1)S(1)} collective-permute-done((bf16[1024,512]{1,0:T(8,128)(2,1)S(1)}, bf16[1024,512]{1,0:T(8,128)(2,1)S(1)}, u32[]{:S(2)}, u32[]{:S(2)}) %collective-permute-start.25) | collective-permute-done | bytes 1048608 | tf_op jit(solution)/shard_map/ppermute | solution.py:198
  226.9 2.4 add_convert_fusion
  235.3 5.2 %collective-permute-done.29 = bf16[256,512]{1,0:T(8,128)(2,1)S(1)} collective-permute-done((bf16[256,512]{1,0:T(8,128)(2,1)S(1)}, bf16[256,512]{1,0:T(8,128)(2,1)S(1)}, u32[]{:S(2)}, u32[]{:S(2)}) %collective-permute-start.29) | collective-permute-done | bytes 262176 | tf_op jit(solution)/shard_map/ppermute | solution.py:241
  242.5 21.1 %collective-permute-done.28 = bf16[256,512]{1,0:T(8,128)(2,1)S(1)} collective-permute-done((bf16[256,512]{1,0:T(8,128)(2,1)S(1)}, bf16[256,512]{1,0:T(8,128)(2,1)S(1)}, u32[]{:S(2)}, u32[]{:S(2)}) %collective-permute-start.28) | collective-permute-done | bytes 262176 | tf_op jit(solution)/shard_map/ppermute | solution.py:241
  263.6 18.0 %collective-permute-start.9 = (bf16[128,2048]{1,0:T(8,128)(2,1)}, bf16[128,2048]{1,0:T(8,128)(2,1)}, u32[]{:S(2)}, u32[]{:S(2)}) collective-permute-start(bf16[128,2048]{1,0:T(8,128)(2,1)} %get-tuple-element.32), channel_id=1, source_target_pairs={{0,16},{4,20},{8,24},{12,28},{16,0},{20,4},{24,8},{28,12},{1,17},{... | collective-permute-start | bytes 1572872 | tf_op jit(solution)/shard_map/ppermute | solution.py:193
  281.6 9.8 %collective-permute-done.27 = bf16[256,512]{1,0:T(8,128)(2,1)S(1)} collective-permute-done((bf16[256,512]{1,0:T(8,128)(2,1)S(1)}, bf16[256,512]{1,0:T(8,128)(2,1)S(1)}, u32[]{:S(2)}, u32[]{:S(2)}) %collective-permute-start.27) | collective-permute-done | bytes 262176 | tf_op jit(solution)/shard_map/ppermute | solution.py:241
  292.5 10.1 %taps.1 = (bf16[256,2048]{1,0:T(8,128)(2,1)}, bf16[256,2048]{1,0:T(8,128)(2,1)}, f32[128,128]{1,0:T(8,128)}) custom-call(s32[1]{0:T(128)} %bitcast.17.turn_ref, bf16[4,256,512]{2,1,0:T(8,128)(2,1)} %pad_maximum_fusion.3.grad_ref, f32[128,2048]{1,0:T(8,128)} %get-tuple-element.17.low_ref, f32[128,2048]{1,0:T(8,128)} %get-tuple-element.18.high_ref, ...), custom_call_target="tpu_custom_call" | custom-call | flops 4294967296 | bytes 8388608 | tf_op jit(solution)/shard_map/taps/pallas_call | solution.py:108
  304.4 2.8 collective-permute-done.8
  307.2 5.2 %fusion.5 = bf16[128,2048]{1,0:T(8,128)(2,1)S(1)} fusion(bf16[2048,2048]{1,0:T(8,128)(2,1)} %copy-done, bf16[128,2048]{1,0:T(8,128)(2,1)S(1)} %collective-permute-done.10, bf16[128,2048]{1,0:T(8,128)(2,1)} %collective-permute-done.9, bf16[128,2048]{1,0:T(8,128)(2,1)} %collective-permute-done.8, bf16[4,128,2048]{2,1,0:T(8,128)(2,1)S(1)} %pad_maximum_fusion, ...), kind=kOutput, calls=%fused_computation.11 | convolution fusion | flops 1075576832 | bytes 11010052 | tf_op jit(solution)/shard_map/dot_general | solution.py:258
  312.4 2.8 collective-permute-start.33
  320.3 8.2 %multiply_convert_fusion = bf16[1024,2048]{1,0:T(8,128)(2,1)} fusion(bf16[1024,2048]{1,0:T(8,128)(2,1)} %collective-permute-done.31, bf16[1024,2048]{1,0:T(8,128)(2,1)S(1)} %copy-done.9, bf16[1024,2048]{1,0:T(8,128)(2,1)S(1)} %copy-done.11), kind=kOutput, calls=%fused_computation | convolution fusion | flops 4303355904 | bytes 14680064 | tf_op jit(solution)/shard_map/dot_general | solution.py:206
  330.1 6.6 %back.1 = (bf16[256,2048]{1,0:T(8,128)(2,1)}, bf16[256,2048]{1,0:T(8,128)(2,1)}) custom-call(f32[128,256]{1,0:T(8,128)} %get-tuple-element.40.base_ref, bf16[256,2048]{1,0:T(8,128)(2,1)} %get-tuple-element.20.grad_conv_ref, bf16[128,2048]{1,0:T(8,128)(2,1)} %copy-done.12, bf16[256,2048]{1,0:T(8,128)(2,1)} %key_ref.1, bf16[256,2048]{1,0:T(8,128)(2,1)} %value_ref.1), custom_call_target="tpu_custom_call" | custom-call | flops 2147483648 | bytes 6291456 | tf_op jit(solution)/shard_map/back/pallas_call | solution.py:161
  (122 shorter events, 57.7 us)
Async XLA Ops:
  3.6 15.5 %collective-permute-start = (bf16[128,2048]{1,0:T(8,128)(2,1)}, bf16[128,2048]{1,0:T(8,128)(2,1)}, u32[]{:S(2)}, u32[]{:S(2)}) collective-permute-start(bf16[128,2048]{1,0:T(8,128)(2,1)} %slice.72), channel_id=1, source_target_pairs={{0,4},{4,8},{8,12},{12,16},{16,20},{20,24},{24,28},{1,5},{5,9},{9,... | collective-permute-start | bytes 1572872 | tf_op jit(solution)/shard_map/ppermute | solution.py:188
  6.7 38.2 %collective-permute-start.20 = (bf16[256,2048]{1,0:T(8,128)(2,1)S(1)}, bf16[256,2048]{1,0:T(8,128)(2,1)}, u32[]{:S(2)}, u32[]{:S(2)}) collective-permute-start(bf16[256,2048]{1,0:T(8,128)(2,1)S(1)} %copy-done.2), channel_id=1, source_target_pairs={{0,8},{4,12},{8,0},{12,4},{16,24},{20,28},{24,16},{28,20},{1,9},{5... | collective-permute-start | bytes 3145736 | tf_op jit(solution)/shard_map/ppermute | solution.py:193
  8.5 52.2 %collective-permute-start.21 = (bf16[256,2048]{1,0:T(8,128)(2,1)S(1)}, bf16[256,2048]{1,0:T(8,128)(2,1)S(1)}, u32[]{:S(2)}, u32[]{:S(2)}) collective-permute-start(bf16[256,2048]{1,0:T(8,128)(2,1)S(1)} %copy-done.2), channel_id=1, source_target_pairs={{0,16},{4,20},{8,24},{12,28},{16,0},{20,4},{24,8},{28,12},{1,17},{... | collective-permute-start | bytes 3145736 | tf_op jit(solution)/shard_map/ppermute | solution.py:193
  10.0 51.5 %collective-permute-start.22 = (bf16[256,2048]{1,0:T(8,128)(2,1)S(1)}, bf16[256,2048]{1,0:T(8,128)(2,1)}, u32[]{:S(2)}, u32[]{:S(2)}) collective-permute-start(bf16[256,2048]{1,0:T(8,128)(2,1)S(1)} %copy-done.2), channel_id=1, source_target_pairs={{0,24},{4,28},{8,16},{12,20},{16,8},{20,12},{24,0},{28,4},{1,25},{... | collective-permute-start | bytes 3145736 | tf_op jit(solution)/shard_map/ppermute | solution.py:193
  16.7 17.3 %collective-permute-start.11 = (bf16[128,2048]{1,0:T(8,128)(2,1)}, bf16[128,2048]{1,0:T(8,128)(2,1)S(1)}, u32[]{:S(2)}, u32[]{:S(2)}) collective-permute-start(bf16[128,2048]{1,0:T(8,128)(2,1)} %get-tuple-element.16), channel_id=1, source_target_pairs={{0,1},{1,2},{2,3},{3,0},{4,5},{5,6},{6,7},{7,4},{8,9},{9,10},{10,1... | collective-permute-start | bytes 1572872 | tf_op jit(solution)/shard_map/ppermute | solution.py:198
  24.6 20.4 %collective-permute-start.1 = (bf16[128,2048]{1,0:T(8,128)(2,1)}, bf16[128,2048]{1,0:T(8,128)(2,1)}, u32[]{:S(2)}, u32[]{:S(2)}) collective-permute-start(bf16[128,2048]{1,0:T(8,128)(2,1)} %get-tuple-element.15), channel_id=1, source_target_pairs={{0,1},{1,2},{2,3},{3,0},{4,5},{5,6},{6,7},{7,4},{8,9},{9,10},{10,1... | collective-permute-start | bytes 1572872 | tf_op jit(solution)/shard_map/ppermute | solution.py:198
  34.0 110.0 %collective-permute-start.4 = (bf16[1024,2048]{1,0:T(8,128)(2,1)}, bf16[1024,2048]{1,0:T(8,128)(2,1)S(1)}, u32[]{:S(2)}, u32[]{:S(2)}) collective-permute-start(bf16[1024,2048]{1,0:T(8,128)(2,1)} %param.10), channel_id=1, source_target_pairs={{0,4},{4,0},{8,12},{12,8},{16,20},{20,16},{24,28},{28,24},{1,5},{5... | collective-permute-start | bytes 12582920 | tf_op jit(solution)/shard_map/ppermute | solution.py:193
  45.0 19.3 %collective-permute-start.12 = (bf16[128,2048]{1,0:T(8,128)(2,1)S(1)}, bf16[128,2048]{1,0:T(8,128)(2,1)S(1)}, u32[]{:S(2)}, u32[]{:S(2)}) collective-permute-start(bf16[128,2048]{1,0:T(8,128)(2,1)S(1)} %collective-permute-done.11), channel_id=1, source_target_pairs={{0,1},{1,2},{2,3},{3,0},{4,5},{5,6},{6,7},{7,4},{8,9},{9,10},{10,1... | collective-permute-start | bytes 1572872 | tf_op jit(solution)/shard_map/ppermute | solution.py:198
  45.0 27.9 %collective-permute-start.2 = (bf16[128,2048]{1,0:T(8,128)(2,1)}, bf16[128,2048]{1,0:T(8,128)(2,1)S(1)}, u32[]{:S(2)}, u32[]{:S(2)}) collective-permute-start(bf16[128,2048]{1,0:T(8,128)(2,1)} %collective-permute-done.1), channel_id=1, source_target_pairs={{0,1},{1,2},{2,3},{3,0},{4,5},{5,6},{6,7},{7,4},{8,9},{9,10},{10,1... | collective-permute-start | bytes 1572872 | tf_op jit(solution)/shard_map/ppermute | solution.py:198
  64.3 32.9 %collective-permute-start.13 = (bf16[128,2048]{1,0:T(8,128)(2,1)S(1)}, bf16[128,2048]{1,0:T(8,128)(2,1)S(1)}, u32[]{:S(2)}, u32[]{:S(2)}) collective-permute-start(bf16[128,2048]{1,0:T(8,128)(2,1)S(1)} %collective-permute-done.12), channel_id=1, source_target_pairs={{0,1},{1,2},{2,3},{3,0},{4,5},{5,6},{6,7},{7,4},{8,9},{9,10},{10,1... | collective-permute-start | bytes 1572872 | tf_op jit(solution)/shard_map/ppermute | solution.py:198
  72.8 21.2 %collective-permute-start.3 = (bf16[128,2048]{1,0:T(8,128)(2,1)S(1)}, bf16[128,2048]{1,0:T(8,128)(2,1)S(1)}, u32[]{:S(2)}, u32[]{:S(2)}) collective-permute-start(bf16[128,2048]{1,0:T(8,128)(2,1)S(1)} %collective-permute-done.2), channel_id=1, source_target_pairs={{0,1},{1,2},{2,3},{3,0},{4,5},{5,6},{6,7},{7,4},{8,9},{9,10},{10,1... | collective-permute-start | bytes 1572872 | tf_op jit(solution)/shard_map/ppermute | solution.py:198
  95.4 14.9 %collective-permute-start.5 = (bf16[128,2048]{1,0:T(8,128)(2,1)S(1)}, bf16[128,2048]{1,0:T(8,128)(2,1)S(1)}, u32[]{:S(2)}, u32[]{:S(2)}) collective-permute-start(bf16[128,2048]{1,0:T(8,128)(2,1)S(1)} %get-tuple-element.24), channel_id=1, source_target_pairs={{0,8},{4,12},{8,0},{12,4},{16,24},{20,28},{24,16},{28,20},{1,9},{5... | collective-permute-start | bytes 1572872 | tf_op jit(solution)/shard_map/ppermute | solution.py:193
  97.5 36.9 %collective-permute-start.6 = (bf16[128,2048]{1,0:T(8,128)(2,1)S(1)}, bf16[128,2048]{1,0:T(8,128)(2,1)S(1)}, u32[]{:S(2)}, u32[]{:S(2)}) collective-permute-start(bf16[128,2048]{1,0:T(8,128)(2,1)S(1)} %get-tuple-element.26), channel_id=1, source_target_pairs={{0,16},{4,20},{8,24},{12,28},{16,0},{20,4},{24,8},{28,12},{1,17},{... | collective-permute-start | bytes 1572872 | tf_op jit(solution)/shard_map/ppermute | solution.py:193
  97.8 51.0 %collective-permute-start.16 = (bf16[128,2048]{1,0:T(8,128)(2,1)S(1)}, bf16[128,2048]{1,0:T(8,128)(2,1)S(1)}, u32[]{:S(2)}, u32[]{:S(2)}) collective-permute-start(bf16[128,2048]{1,0:T(8,128)(2,1)S(1)} %get-tuple-element.28), channel_id=1, source_target_pairs={{0,24},{4,28},{8,16},{12,20},{16,8},{20,12},{24,0},{28,4},{1,25},{... | collective-permute-start | bytes 1572872 | tf_op jit(solution)/shard_map/ppermute | solution.py:193
  99.6 34.9 %collective-permute-start.7 = (bf16[128,2048]{1,0:T(8,128)(2,1)S(1)}, bf16[128,2048]{1,0:T(8,128)(2,1)S(1)}, u32[]{:S(2)}, u32[]{:S(2)}) collective-permute-start(bf16[128,2048]{1,0:T(8,128)(2,1)S(1)} %get-tuple-element.25), channel_id=1, source_target_pairs={{0,24},{4,28},{8,16},{12,20},{16,8},{20,12},{24,0},{28,4},{1,25},{... | collective-permute-start | bytes 1572872 | tf_op jit(solution)/shard_map/ppermute | solution.py:193
  110.4 33.6 %collective-permute-start.15 = (bf16[128,2048]{1,0:T(8,128)(2,1)S(1)}, bf16[128,2048]{1,0:T(8,128)(2,1)S(1)}, u32[]{:S(2)}, u32[]{:S(2)}) collective-permute-start(bf16[128,2048]{1,0:T(8,128)(2,1)S(1)} %get-tuple-element.29), channel_id=1, source_target_pairs={{0,16},{4,20},{8,24},{12,28},{16,0},{20,4},{24,8},{28,12},{1,17},{... | collective-permute-start | bytes 1572872 | tf_op jit(solution)/shard_map/ppermute | solution.py:193
  148.6 25.5 %collective-permute-start.23 = (bf16[1024,512]{1,0:T(8,128)(2,1)S(1)}, bf16[1024,512]{1,0:T(8,128)(2,1)S(1)}, u32[]{:S(2)}, u32[]{:S(2)}) collective-permute-start(bf16[1024,512]{1,0:T(8,128)(2,1)S(1)} %fusion.26), channel_id=1, source_target_pairs={{0,1},{1,2},{2,3},{3,0},{4,5},{5,6},{6,7},{7,4},{8,9},{9,10},{10,1... | collective-permute-start | bytes 3145736 | tf_op jit(solution)/shard_map/ppermute | solution.py:198
  155.2 165.1 %collective-permute-start.31 = (bf16[1024,2048]{1,0:T(8,128)(2,1)}, bf16[1024,2048]{1,0:T(8,128)(2,1)}, u32[]{:S(2)}, u32[]{:S(2)}) collective-permute-start(bf16[1024,2048]{1,0:T(8,128)(2,1)} %convolution_convert_fusion), channel_id=1, source_target_pairs={{0,4},{4,0},{8,12},{12,8},{16,20},{20,16},{24,28},{28,24},{1,5},{5... | collective-permute-start | bytes 12582920 | tf_op jit(solution)/shard_map/ppermute | solution.py:193
  176.4 24.4 %collective-permute-start.24 = (bf16[1024,512]{1,0:T(8,128)(2,1)S(1)}, bf16[1024,512]{1,0:T(8,128)(2,1)S(1)}, u32[]{:S(2)}, u32[]{:S(2)}) collective-permute-start(bf16[1024,512]{1,0:T(8,128)(2,1)S(1)} %add_convert_fusion.2), channel_id=1, source_target_pairs={{0,1},{1,2},{2,3},{3,0},{4,5},{5,6},{6,7},{7,4},{8,9},{9,10},{10,1... | collective-permute-start | bytes 3145736 | tf_op jit(solution)/shard_map/ppermute | solution.py:198
  180.1 51.1 %collective-permute-start.19 = (bf16[128,2048]{1,0:T(8,128)(2,1)S(1)}, bf16[128,2048]{1,0:T(8,128)(2,1)S(1)}, u32[]{:S(2)}, u32[]{:S(2)}) collective-permute-start(bf16[128,2048]{1,0:T(8,128)(2,1)S(1)} %get-tuple-element.34), channel_id=1, source_target_pairs={{0,24},{4,28},{8,16},{12,20},{16,8},{20,12},{24,0},{28,4},{1,25},{... | collective-permute-start | bytes 1572872 | tf_op jit(solution)/shard_map/ppermute | solution.py:193
  181.8 50.8 %collective-permute-start.18 = (bf16[128,2048]{1,0:T(8,128)(2,1)S(1)}, bf16[128,2048]{1,0:T(8,128)(2,1)S(1)}, u32[]{:S(2)}, u32[]{:S(2)}) collective-permute-start(bf16[128,2048]{1,0:T(8,128)(2,1)S(1)} %get-tuple-element.35), channel_id=1, source_target_pairs={{0,16},{4,20},{8,24},{12,28},{16,0},{20,4},{24,8},{28,12},{1,17},{... | collective-permute-start | bytes 1572872 | tf_op jit(solution)/shard_map/ppermute | solution.py:193
  182.8 50.2 %collective-permute-start.17 = (bf16[128,2048]{1,0:T(8,128)(2,1)S(1)}, bf16[128,2048]{1,0:T(8,128)(2,1)S(1)}, u32[]{:S(2)}, u32[]{:S(2)}) collective-permute-start(bf16[128,2048]{1,0:T(8,128)(2,1)S(1)} %get-tuple-element.33), channel_id=1, source_target_pairs={{0,8},{4,12},{8,0},{12,4},{16,24},{20,28},{24,16},{28,20},{1,9},{5... | collective-permute-start | bytes 1572872 | tf_op jit(solution)/shard_map/ppermute | solution.py:193
  203.2 23.7 %collective-permute-start.25 = (bf16[1024,512]{1,0:T(8,128)(2,1)S(1)}, bf16[1024,512]{1,0:T(8,128)(2,1)S(1)}, u32[]{:S(2)}, u32[]{:S(2)}) collective-permute-start(bf16[1024,512]{1,0:T(8,128)(2,1)S(1)} %add_convert_fusion.1), channel_id=1, source_target_pairs={{0,1},{1,2},{2,3},{3,0},{4,5},{5,6},{6,7},{7,4},{8,9},{9,10},{10,1... | collective-permute-start | bytes 3145736 | tf_op jit(solution)/shard_map/ppermute | solution.py:198
  229.4 11.2 %collective-permute-start.29 = (bf16[256,512]{1,0:T(8,128)(2,1)S(1)}, bf16[256,512]{1,0:T(8,128)(2,1)S(1)}, u32[]{:S(2)}, u32[]{:S(2)}) collective-permute-start(bf16[256,512]{1,0:T(8,128)(2,1)S(1)} %bitcast.70), channel_id=1, source_target_pairs={{0,24},{1,16},{2,8},{3,0},{4,28},{5,20},{6,12},{7,4},{8,25},{9,17}... | collective-permute-start | bytes 786440 | tf_op jit(solution)/shard_map/ppermute | solution.py:241
  231.2 32.4 %collective-permute-start.28 = (bf16[256,512]{1,0:T(8,128)(2,1)S(1)}, bf16[256,512]{1,0:T(8,128)(2,1)S(1)}, u32[]{:S(2)}, u32[]{:S(2)}) collective-permute-start(bf16[256,512]{1,0:T(8,128)(2,1)S(1)} %bitcast.69), channel_id=1, source_target_pairs={{0,16},{1,24},{2,0},{3,8},{4,20},{5,28},{6,4},{7,12},{8,17},{9,25}... | collective-permute-start | bytes 786440 | tf_op jit(solution)/shard_map/ppermute | solution.py:241
  232.5 58.9 %collective-permute-start.27 = (bf16[256,512]{1,0:T(8,128)(2,1)S(1)}, bf16[256,512]{1,0:T(8,128)(2,1)S(1)}, u32[]{:S(2)}, u32[]{:S(2)}) collective-permute-start(bf16[256,512]{1,0:T(8,128)(2,1)S(1)} %bitcast.68), channel_id=1, source_target_pairs={{0,8},{1,0},{2,24},{3,16},{4,12},{5,4},{6,28},{7,20},{8,9},{9,1},{... | collective-permute-start | bytes 786440 | tf_op jit(solution)/shard_map/ppermute | solution.py:241
  233.0 58.4 %collective-permute-start.26 = (bf16[256,512]{1,0:T(8,128)(2,1)S(1)}, bf16[256,512]{1,0:T(8,128)(2,1)S(1)}, u32[]{:S(2)}, u32[]{:S(2)}) collective-permute-start(bf16[256,512]{1,0:T(8,128)(2,1)S(1)} %bitcast.67), channel_id=1, source_target_pairs={{0,0},{1,8},{2,16},{3,24},{4,4},{5,12},{6,20},{7,28},{8,1},{9,9},{... | collective-permute-start | bytes 786440 | tf_op jit(solution)/shard_map/ppermute | solution.py:241
  240.6 62.2 %collective-permute-start.10 = (bf16[128,2048]{1,0:T(8,128)(2,1)}, bf16[128,2048]{1,0:T(8,128)(2,1)S(1)}, u32[]{:S(2)}, u32[]{:S(2)}) collective-permute-start(bf16[128,2048]{1,0:T(8,128)(2,1)} %get-tuple-element.31), channel_id=1, source_target_pairs={{0,24},{4,28},{8,16},{12,20},{16,8},{20,12},{24,0},{28,4},{1,25},{... | collective-permute-start | bytes 1572872 | tf_op jit(solution)/shard_map/ppermute | solution.py:193
  263.6 40.7 %collective-permute-start.9 = (bf16[128,2048]{1,0:T(8,128)(2,1)}, bf16[128,2048]{1,0:T(8,128)(2,1)}, u32[]{:S(2)}, u32[]{:S(2)}) collective-permute-start(bf16[128,2048]{1,0:T(8,128)(2,1)} %get-tuple-element.32), channel_id=1, source_target_pairs={{0,16},{4,20},{8,24},{12,28},{16,0},{20,4},{24,8},{28,12},{1,17},{... | collective-permute-start | bytes 1572872 | tf_op jit(solution)/shard_map/ppermute | solution.py:193
  291.4 15.8 %collective-permute-start.8 = (bf16[128,2048]{1,0:T(8,128)(2,1)}, bf16[128,2048]{1,0:T(8,128)(2,1)}, u32[]{:S(2)}, u32[]{:S(2)}) collective-permute-start(bf16[128,2048]{1,0:T(8,128)(2,1)} %get-tuple-element.30), channel_id=1, source_target_pairs={{0,8},{4,12},{8,0},{12,4},{16,24},{20,28},{24,16},{28,20},{1,9},{5... | collective-permute-start | bytes 1572872 | tf_op jit(solution)/shard_map/ppermute | solution.py:193
  316.3 13.0 %collective-permute-start.30 = (bf16[128,2048]{1,0:T(8,128)(2,1)S(1)}, bf16[128,2048]{1,0:T(8,128)(2,1)S(1)}, u32[]{:S(2)}, u32[]{:S(2)}) collective-permute-start(bf16[128,2048]{1,0:T(8,128)(2,1)S(1)} %slice.69), channel_id=1, source_target_pairs={{4,0},{8,4},{12,8},{16,12},{20,16},{24,20},{28,24},{5,1},{9,5},{13... | collective-permute-start | bytes 1572872 | tf_op jit(solution)/shard_map/ppermute | solution.py:188
  318.1 10.4 %collective-permute-start.34 = (f32[128,128]{1,0:T(8,128)S(1)}, f32[128,128]{1,0:T(8,128)S(1)}, u32[]{:S(2)}, u32[]{:S(2)}) collective-permute-start(f32[128,128]{1,0:T(8,128)S(1)} %add.162), channel_id=1, source_target_pairs={{0,16},{4,20},{8,24},{12,28},{16,0},{20,4},{24,8},{28,12},{1,17},{... | collective-permute-start | bytes 196616 | tf_op jit(solution)/shard_map/ppermute | solution.py:193
  (18 other events, 385.3 us)

commit v2 on v1

v2 whole, which is shorter than its diff:
```python
import functools
import math

import jax
import jax.numpy as jnp
from jax import lax
from jax.experimental import pallas as pl
from jax.experimental.pallas import tpu as pltpu
from jax.sharding import PartitionSpec as P

LANES = 128
STEP = 512
GRANT = 58 * 1024 * 1024
f32 = jnp.float32
bf16 = jnp.bfloat16


def band(base, index, span):
    row = jnp.broadcast_to(base[index : index + 1], (span, 2 * span))
    return pltpu.roll(row, 0, 1, stride=1, stride_axis=0).astype(bf16)


def banded(base, column, first, owner, span, group):
    total = jnp.zeros(owner.shape, f32)
    for g in range(LANES // group):
        value = jnp.dot(band(base, first + g, span), column, preferred_element_type=f32)
        total = jnp.where(owner == g, value, total)
    return total


def conv_kernel(span, group, turn_ref, base_ref, rim_ref, product_ref, query_ref, *refs):
    gated_ref, conv_ref = refs[-2:]
    owner = lax.broadcasted_iota(jnp.int32, (span, 2 * LANES), 1) % LANES // group
    for start in range(0, query_ref.shape[1], LANES):
        cut = slice(start, start + LANES)
        late = product_ref[:, cut]
        early = jnp.concatenate([rim_ref[:, cut], late[:span]], 0)
        column = jnp.concatenate([early, late], 1)
        total = banded(base_ref[...], column, start // group, owner, span, group)
        conv = jnp.concatenate([total[:, :LANES], total[:, LANES:]], 0)
        conv_ref[:, cut] = conv
        gated_ref[:, cut] = (query_ref[:, cut].astype(f32) * conv).astype(bf16)


def conv_call(turn, base, rim, product, query, after, span, group):
    tokens, width = query.shape
    lanes = min(width, STEP)

    def block(rows):
        return pl.BlockSpec((rows, lanes), lambda i, turn: (0, i))

    return pl.pallas_call(
        functools.partial(conv_kernel, span, group),
        grid_spec=pltpu.PrefetchScalarGridSpec(
            num_scalar_prefetch=1,
            grid=(width // lanes,),
            in_specs=[
                pl.BlockSpec((lanes // group, 2 * span), lambda i, turn: (i, 0)),
                block(span),
                block(tokens),
                block(tokens),
            ]
            + [pl.BlockSpec(memory_space=pl.ANY)] * len(after),
            out_specs=[
                pl.BlockSpec((tokens, lanes), lambda i, turn: (0, i ^ turn[0])),
                block(tokens),
            ],
        ),
        out_shape=[
            jax.ShapeDtypeStruct((tokens, width), bf16),
            jax.ShapeDtypeStruct((tokens, width), f32),
        ],
        cost_estimate=pl.CostEstimate(
            flops=4 * span * tokens * width * LANES // group,
            bytes_accessed=12 * tokens * width,
            transcendentals=0,
        ),
        name="conv",
    )(turn, base, rim, product, query, *after)


def gate_kernel(span, turn_ref, grad_ref, conv_ref, query_ref, query_grad_ref, grad_conv_ref, grad_rim_ref):
    grad = grad_ref[...].astype(f32)
    query_grad_ref[...] = (grad * conv_ref[...]).astype(bf16)
    grad_conv = (grad * query_ref[...].astype(f32)).astype(bf16)
    grad_conv_ref[...] = grad_conv
    grad_rim_ref[...] = grad_conv[:span]


def gate_call(turn, grad, conv, query, span):
    tokens, width = query.shape
    lanes = min(width, STEP)

    def block(rows):
        return pl.BlockSpec((rows, lanes), lambda i, turn: (0, i))

    return pl.pallas_call(
        functools.partial(gate_kernel, span),
        grid_spec=pltpu.PrefetchScalarGridSpec(
            num_scalar_prefetch=1,
            grid=(width // lanes,),
            in_specs=[
                pl.BlockSpec((tokens, lanes), lambda i, turn: (0, i ^ turn[0])),
                block(tokens),
                block(tokens),
            ],
            out_specs=[block(tokens), block(tokens), block(span)],
        ),
        out_shape=[
            jax.ShapeDtypeStruct((tokens, width), bf16),
            jax.ShapeDtypeStruct((tokens, width), bf16),
            jax.ShapeDtypeStruct((span, width), bf16),
        ],
        cost_estimate=pl.CostEstimate(flops=2 * tokens * width, bytes_accessed=12 * tokens * width, transcendentals=0),
        name="gate",
    )(turn, grad, conv, query)


def taps_kernel(span, group, grad_conv_ref, rim_ref, product_ref, *refs):
    taps_ref = refs[-1]
    rows = lax.broadcasted_iota(jnp.int32, (span, span), 0)
    columns = lax.broadcasted_iota(jnp.int32, (span, span), 1)
    flip = jnp.where(rows + columns == span - 1, 1.0, 0.0).astype(bf16)
    owner = lax.broadcasted_iota(jnp.int32, (span, 2 * LANES), 1) % LANES // group
    for start in range(0, grad_conv_ref.shape[1], LANES):
        cut = slice(start, start + LANES)
        grad_conv = grad_conv_ref[:, cut]
        left = jnp.concatenate([grad_conv[:span], grad_conv[span:]], 1)
        left = jnp.dot(flip, left, preferred_element_type=f32).astype(bf16)
        late = product_ref[:, cut]
        early = jnp.concatenate([rim_ref[:, cut], late[:span]], 0)
        right = jnp.concatenate([early, late], 1)
        for g in range(LANES // group):
            one = jnp.where(owner == g, left, jnp.zeros_like(left))
            corr = lax.dot_general(one, right, (((1,), (1,)), ((), ())), preferred_element_type=f32)
            lined = pltpu.roll(corr, 0, 1, stride=1, stride_axis=0)
            at = start // group + g
            taps_ref[at : at + 1] = jnp.sum(lined[:, span:], axis=0, keepdims=True)


def taps_call(grad_conv, rim, product, after, span, group):
    tokens, width = grad_conv.shape
    lanes = min(width, STEP)

    def block(rows):
        return pl.BlockSpec((rows, lanes), lambda i: (0, i))

    return pl.pallas_call(
        functools.partial(taps_kernel, span, group),
        grid=(width // lanes,),
        in_specs=[block(tokens), block(span), block(tokens)] + [pl.BlockSpec(memory_space=pl.ANY)] * len(after),
        out_specs=pl.BlockSpec((lanes // group, span), lambda i: (i, 0)),
        out_shape=jax.ShapeDtypeStruct((width // group, span), f32),
        cost_estimate=pl.CostEstimate(
            flops=8 * span * tokens * width * LANES // group,
            bytes_accessed=5 * tokens * width,
            transcendentals=0,
        ),
        name="taps",
    )(grad_conv, rim, product, *after)


def back_kernel(span, group, base_ref, grad_conv_ref, rim_ref, key_ref, value_ref, *refs):
    key_grad_ref, value_grad_ref = refs[-2:]
    owner = lax.broadcasted_iota(jnp.int32, (span, 2 * LANES), 1) % LANES // group
    for start in range(0, key_ref.shape[1], LANES):
        cut = slice(start, start + LANES)
        here = grad_conv_ref[:, cut]
        after = jnp.concatenate([here[span:], rim_ref[:, cut]], 0)
        column = jnp.concatenate([here, after], 1)
        total = banded(base_ref[...], column, start // group, owner, span, group)
        product = jnp.concatenate([total[:, :LANES], total[:, LANES:]], 0)
        key_grad_ref[:, cut] = (product * value_ref[:, cut].astype(f32)).astype(bf16)
        value_grad_ref[:, cut] = (product * key_ref[:, cut].astype(f32)).astype(bf16)


def back_call(base, grad_conv, rim, key, value, after, span, group):
    tokens, width = key.shape
    lanes = min(width, STEP)

    def block(rows):
        return pl.BlockSpec((rows, lanes), lambda i: (0, i))

    return pl.pallas_call(
        functools.partial(back_kernel, span, group),
        grid=(width // lanes,),
        in_specs=[
            pl.BlockSpec((lanes // group, 2 * span), lambda i: (i, 0)),
            block(tokens),
            block(span),
            block(tokens),
            block(tokens),
        ]
        + [pl.BlockSpec(memory_space=pl.ANY)] * len(after),
        out_specs=[block(tokens), block(tokens)],
        out_shape=[
            jax.ShapeDtypeStruct((tokens, width), bf16),
            jax.ShapeDtypeStruct((tokens, width), bf16),
        ],
        cost_estimate=pl.CostEstimate(
            flops=4 * span * tokens * width * LANES // group,
            bytes_accessed=12 * tokens * width,
            transcendentals=0,
        ),
        name="back",
    )(base, grad_conv, rim, key, value, *after)


def from_behind(shard, by):
    size = lax.axis_size("row")
    pairs = [(i, i + by) for i in range(size) if 0 <= i + by < size]
    return lax.ppermute(shard, "row", pairs)


def exchange(shard, bits):
    size = lax.axis_size("row")
    return lax.ppermute(shard, "row", [(i, i ^ bits) for i in range(size)])


def ring(shard):
    size = lax.axis_size("col")
    return lax.ppermute(shard, "col", [(i, (i + 1) % size) for i in range(size)])


def dot_nt(a, b):
    return lax.dot_general(a, b, (((1,), (1,)), ((), ())), preferred_element_type=f32)


def dot_tn(a, b):
    return lax.dot_general(a, b, (((0,), (0,)), ((), ())), preferred_element_type=f32)


def keep_kernel(*refs):
    pass


def once(array, *others):
    anywhere = pl.BlockSpec(memory_space=pl.ANY)
    return pl.pallas_call(
        keep_kernel,
        in_specs=[anywhere] * (1 + len(others)),
        out_specs=anywhere,
        out_shape=jax.ShapeDtypeStruct(array.shape, array.dtype),
        input_output_aliases={0: 0},
        name="once",
    )(array, *others)


def pick_kernel(at_ref, *refs):
    pieces, out_ref = refs[:4], refs[-1]
    for place, piece in enumerate(pieces):

        @pl.when(at_ref[0] == place)
        def _(piece=piece):
            pltpu.sync_copy(piece, out_ref)


def pick(pieces, at):
    return pl.pallas_call(
        pick_kernel,
        in_specs=[pl.BlockSpec(memory_space=pltpu.SMEM)] + [pl.BlockSpec(memory_space=pl.ANY)] * 4,
        out_specs=pl.BlockSpec(memory_space=pltpu.VMEM),
        out_shape=jax.ShapeDtypeStruct(pieces[0].shape, pieces[0].dtype),
        cost_estimate=pl.CostEstimate(flops=0, bytes_accessed=4 * pieces[0].size, transcendentals=0),
        name="pick",
    )(at.astype(jnp.int32).reshape(1), *pieces)


def copy_kernel(at_ref, in_ref, out_ref):
    out_ref[...] = in_ref[0]


def take(stack, at):
    _, rows, columns = stack.shape
    part = rows // 4
    return pl.pallas_call(
        copy_kernel,
        grid_spec=pltpu.PrefetchScalarGridSpec(
            num_scalar_prefetch=1,
            grid=(4,),
            in_specs=[pl.BlockSpec((1, part, columns), lambda i, at: (at[0], i, 0))],
            out_specs=pl.BlockSpec((part, columns), lambda i, at: (i, 0)),
        ),
        out_shape=jax.ShapeDtypeStruct((rows, columns), stack.dtype),
        cost_estimate=pl.CostEstimate(flops=0, bytes_accessed=4 * rows * columns, transcendentals=0),
        name="take",
    )(at.astype(jnp.int32).reshape(1), stack)


def add_kernel(parts, at_ref, *refs):
    pieces, came = refs[:4], refs[4]
    out_ref, held_ref, came_ref, sems = refs[-4:]
    rows = held_ref.shape[0] // parts

    def copies(source, target, which):
        for part in range(parts):
            cut = pl.ds(part * rows, rows)
            yield pltpu.make_async_copy(source.at[cut], target.at[cut], sems.at[which, part])

    for place, piece in enumerate(pieces):

        @pl.when(at_ref[0] == place)
        def _(piece=piece):
            pairs = list(zip(copies(piece, held_ref, 0), copies(came, came_ref, 1)))
            for one, other in pairs:
                one.start()
                other.start()
            for part, (one, other) in enumerate(pairs):
                one.wait()
                other.wait()
                cut = slice(part * rows, (part + 1) * rows)
                out_ref[cut] = (held_ref[cut].astype(f32) + came_ref[cut].astype(f32)).astype(bf16)


def pick_and_add(pieces, at, came, after):
    anywhere = pl.BlockSpec(memory_space=pl.ANY)
    parts = 4
    return pl.pallas_call(
        functools.partial(add_kernel, parts),
        in_specs=[pl.BlockSpec(memory_space=pltpu.SMEM)] + [anywhere] * (5 + len(after)),
        out_specs=pl.BlockSpec(memory_space=pltpu.VMEM),
        out_shape=jax.ShapeDtypeStruct(came.shape, bf16),
        scratch_shapes=[
            pltpu.VMEM(came.shape, bf16),
            pltpu.VMEM(came.shape, bf16),
            pltpu.SemaphoreType.DMA((2, parts)),
        ],
        cost_estimate=pl.CostEstimate(flops=came.size, bytes_accessed=6 * came.size, transcendentals=0),
        name="add",
    )(at.astype(jnp.int32).reshape(1), *pieces, came, *after)


def product_kernel(count, gradient, *refs):
    pieces, (own_ref, other_ref) = refs[:count], refs[count : count + 2]
    left_ref = refs[-1]
    step = pl.program_id(0)

    @pl.when(step == 0)
    def _():
        at = 0
        for piece in pieces:
            left_ref[at : at + piece.shape[0]] = piece[...]
            at += piece.shape[0]

    def write(value):
        at = 0
        for out in refs[-1 - gradient[1] : -1]:
            out[...] = value[at : at + out.shape[0]].astype(bf16)
            at += out.shape[0]

    if gradient[0]:
        steps = pl.num_programs(0) // 2

        @pl.when(step < steps)
        def _():
            write(dot_nt(left_ref[...], own_ref[...]))

        @pl.when(step >= steps)
        def _():
            write(dot_nt(left_ref[...], other_ref[...]))
    else:
        half = own_ref.shape[0]
        value = jnp.dot(left_ref[:, :half], own_ref[...], preferred_element_type=f32)
        value = value + jnp.dot(left_ref[:, half:], other_ref[...], preferred_element_type=f32)
        write(value)


def product_call(pieces, own, other, after, outs, gradient):
    block = 256
    rows = sum(piece.shape[0] for piece in pieces)
    depth = pieces[0].shape[1]
    if gradient:
        count = own.shape[0] // block
        columns = 2 * own.shape[0]
        specs = [
            pl.BlockSpec((block, depth), lambda i: (jnp.minimum(i, count - 1), 0)),
            pl.BlockSpec((block, depth), lambda i: (jnp.maximum(i - count, 0), 0)),
        ]
    else:
        columns = own.shape[1]
        specs = [pl.BlockSpec((own.shape[0], block), lambda i: (0, i))] * 2
    return list(
        pl.pallas_call(
            functools.partial(product_kernel, len(pieces), (gradient, outs)),
            grid=(columns // block,),
            in_specs=[pl.BlockSpec(piece.shape, lambda i: (0, 0)) for piece in pieces]
            + specs
            + [pl.BlockSpec(memory_space=pl.ANY)] * len(after),
            out_specs=[pl.BlockSpec((rows // outs, block), lambda i: (0, i))] * outs,
            out_shape=[jax.ShapeDtypeStruct((rows // outs, columns), bf16)] * outs,
            scratch_shapes=[pltpu.VMEM((rows, depth), bf16)],
            compiler_params=pltpu.CompilerParams(vmem_limit_bytes=GRANT),
            cost_estimate=pl.CostEstimate(
                flops=2 * rows * depth * columns,
                bytes_accessed=2 * (rows * depth + depth * columns + rows * columns),
                transcendentals=0,
            ),
            name="product",
        )(*pieces, own, other, *after)
    )


def weight_kernel(pieces, scale, *refs):
    held, grads, came = refs[:4], refs[4 : 4 + pieces], refs[4 + pieces : 8 + pieces]
    right_ref = refs[-1]
    step = pl.program_id(0)

    @pl.when(step == 0)
    def _():
        at = 0
        for piece in grads:
            right_ref[at : at + piece.shape[0]] = piece[...]
            at += piece.shape[0]

    left = jnp.concatenate([piece[...] for piece in held], 0)
    value = dot_tn(left, right_ref[...])
    if scale is None:
        for place, out_ref in enumerate(refs[-5:-1]):

            @pl.when(step == place)
            def _(out_ref=out_ref):
                out_ref[...] = value.astype(bf16)
    else:
        for place, came_ref in enumerate(came):

            @pl.when(step == place)
            def _(came_ref=came_ref):
                refs[-2][...] = ((value + came_ref[...].astype(f32)) * scale).astype(bf16)


def weight_call(held, grads, came, after, first, scale):
    width, columns = held[0].shape[1] // 2, grads[0].shape[1]
    block = width // 4
    tokens = held[0].shape[0]
    rows = tokens * len(held)
    return pl.pallas_call(
        functools.partial(weight_kernel, len(grads), scale),
        grid=(width // block,),
        in_specs=[pl.BlockSpec((tokens, block), lambda i: (0, first // block + i))] * len(held)
        + [pl.BlockSpec(piece.shape, lambda i: (0, 0)) for piece in grads]
        + [pl.BlockSpec((block, columns), lambda i: (0, 0))] * len(came)
        + [pl.BlockSpec(memory_space=pl.ANY)] * len(after),
        out_specs=pl.BlockSpec((block, columns), lambda i: (i, 0))
        if came
        else [pl.BlockSpec((block, columns), lambda i: (0, 0))] * 4,
        out_shape=jax.ShapeDtypeStruct((width, columns), bf16)
        if came
        else [jax.ShapeDtypeStruct((block, columns), bf16)] * 4,
        scratch_shapes=[pltpu.VMEM((rows, columns), bf16)],
        compiler_params=pltpu.CompilerParams(vmem_limit_bytes=GRANT),
        cost_estimate=pl.CostEstimate(
            flops=2 * rows * width * columns,
            bytes_accessed=2 * rows * (width + columns) + 4 * width * columns,
            transcendentals=0,
        ),
        name="weight",
    )(*held, *grads, *came, *after)


def projection(gated, out_weight, other_weight, out_grad, neighbours, total_tokens):
    chip = lax.axis_index("row") // 2
    plane = lax.axis_index("col")
    tokens = gated.shape[0]
    half, part = out_weight.shape[0], tokens // 2
    weights = (out_weight, other_weight)

    panel = lax.all_gather(gated, "col")
    kept = product_call([out_grad], *weights, [gated], 1, True)[0]
    grad_x, grad_y = [once(piece, kept) for piece in neighbours]
    far_x, far_y = grad_x[:part], grad_y[part:]
    far = [exchange(far_x, 4), exchange(far_y, 2)]
    grads = [out_grad, grad_x, grad_y, *far]

    to_x = product_call([grad_x], *weights, [far_x, far_y], 1, True)[0]
    to_y = product_call([grad_y], *weights, [to_x], 1, True)[0]
    to_far = product_call(far, *weights, [to_y], 1, True)[0]
    back_x, back_y = exchange(to_x, 2), exchange(to_y, 4)
    partial = [kept, back_x, back_y, exchange(to_far, 6)]

    def add(step, total, *after):
        return pick_and_add(partial, chip ^ (plane + 7 - step) % 4, ring(total), after)

    first = add(1, pick(partial, chip ^ (plane + 3) % 4))

    held = [take(panel, chip ^ d) for d in range(4)]
    held_x, held_y = exchange(held[1], 2), exchange(held[2], 4)
    held_far = exchange(once(held[3], held_x, held_y), 6)
    near = product_call([held_x, held_y], *weights, [first], 2, False)
    mixed_x, mixed_y = exchange(near[0], 2), exchange(near[1], 4)
    second = add(2, first, near[0])
    last = product_call([held[0], held_far], *weights, [near[0], second], 2, False)
    mixed_far = exchange(last[1], 6)
    held = [held[0], held_x, held_y, held_far]
    sent = weight_call(held, grads, [], [last[0], second], half, None)
    third = add(3, second, *sent[:1], mixed_x, mixed_y)
    mixed = (last[0].astype(f32) + mixed_x.astype(f32) + mixed_y.astype(f32) + mixed_far.astype(f32)).astype(bf16)

    came = [exchange(block, 1) for block in sent]

    def weight_half(after):
        return weight_call(held, grads, came, after, 0, 1.0 / math.sqrt(total_tokens))

    return mixed, third, weight_half


def projection_gathered(gated, out_weight, _, out_grad, neighbours, total_tokens):
    panel = lax.all_gather(gated, "col", axis=1, tiled=True)
    weights = lax.all_gather(out_weight, "row", axis=0, tiled=True)
    mixed = jnp.dot(panel, weights, preferred_element_type=f32).astype(bf16)
    partial = dot_nt(out_grad, weights).astype(bf16)
    grad_gated = lax.psum_scatter(partial, "col", scatter_dimension=1, tiled=True)
    weight_sum = lax.psum_scatter(
        dot_tn(panel, out_grad).astype(bf16), "row", scatter_dimension=0, tiled=True
    ).astype(f32)
    weight_grad = (weight_sum * (1.0 / math.sqrt(total_tokens))).astype(bf16)
    return mixed, grad_gated, lambda after: weight_grad


def shards(query_in, key_in, value_in, filters, out_weight, out_grad):
    tokens, width = query_in.shape
    groups, span = filters.shape
    group = width // groups
    rows, cols = lax.axis_size("row"), lax.axis_size("col")
    total_tokens = tokens * rows
    paired = rows == 2 * cols and cols == 4 and width == 2 * out_weight.shape[0] and width % (2 * STEP) == 0
    core = lax.axis_index("row") % 2
    turn = core * (width // STEP // 2) if paired else core * 0
    turn = turn.astype(jnp.int32).reshape(1)

    product = (key_in.astype(f32) * value_in.astype(f32)).astype(bf16)
    rim = from_behind(product[-span:], 1)
    zeros = jnp.zeros((groups, span - 1), f32)
    causal = jnp.concatenate([zeros[:, :1], filters[:, ::-1], zeros], 1)
    anticausal = jnp.concatenate([filters, zeros, zeros[:, :1]], 1)
    other_weight = exchange(out_weight, 1) if paired else product
    neighbours = []
    if paired:
        neighbours = [exchange(out_grad, 2), exchange(out_grad, 4)]
    gated, conv = conv_call(turn, causal, rim, product, query_in, [other_weight], span, group)

    project = projection if paired else projection_gathered
    mixed, grad_gated, weight_half = project(gated, out_weight, other_weight, out_grad, neighbours, total_tokens)

    query_grad, grad_conv, grad_rim = gate_call(turn, grad_gated, conv, query_in, span)
    grad_rim = from_behind(grad_rim, -1)
    taps = taps_call(grad_conv, rim, product, [], span, group)
    weight_grad = weight_half([taps])
    taps = taps + once(exchange(taps, 1), weight_grad)
    key_grad, value_grad = back_call(anticausal, grad_conv, grad_rim, key_in, value_in, [taps], span, group)
    taps = taps + once(exchange(taps, 2), key_grad)
    bits = 4
    while bits < rows:
        taps = taps + exchange(taps, bits)
        bits *= 2
    filter_grad = taps[:, ::-1] * (1.0 / math.sqrt(total_tokens * group))
    return (mixed, query_grad, key_grad, value_grad, weight_grad, filter_grad)


def solution(mesh):
    placed = (
        P("row", "col"),
        P("row", "col"),
        P("row", "col"),
        P("col", None),
        P("row", "col"),
        P("row", "col"),
    )
    return jax.shard_map(
        shards,
        mesh=mesh,
        in_specs=placed,
        out_specs=(
            P("row", "col"),
            P("row", "col"),
            P("row", "col"),
            P("row", "col"),
            P("row", "col"),
            P("col", None),
        ),
        check_vma=False,
    )
```

time: 337 us -> 269 us (0.80)
  waiting for transfers between devices: 187 us -> 65.6 us
  Pallas kernels: 27.7 us -> 129 us
  matrix products: 37.8 us -> 0 us
  starting transfers between devices: 53.6 us -> 34.7 us
  between operations: 1.11 us -> 14.3 us
  local copies, waits for them, and re-layouts: 21.8 us -> 14.5 us
    pallas_call x1 -> x23, Pallas kernels: 10.1 us -> 116 us  [the longest x6 57.1 us: product_call(): pl.pallas_call(functools.partial(product_kernel, len(pieces), (gradient,...]
    ppermute x9 -> x3, waiting for transfers between devices: 92.9 us -> 12.6 us  [ring(): lax.ppermute(shard, 'col', [(i, (i + 1) % size) for i in range(size)])]
    dot_general x10 -> x0, matrix products: 37.8 us -> none  [the longest x2 14.5 us: dot_tn(): lax.dot_general(a, b, (((0,), (0,)), ((), ())), preferred_element_type=f32)]
    ppermute x4 -> x0, waiting for transfers between devices: 36.1 us -> none  [projection(): lax.ppermute(piece.reshape(blocks * span, lanes), ('row', 'col'), pairs)]
    ppermute x20 -> x21, starting transfers between devices: 38.7 us -> 28.4 us  [exchange(): return lax.ppermute(shard, 'row', [(i, i ^ bits) for i in range(size)])]
    ppermute x20 -> x21, waiting for transfers between devices: 58.4 us -> 50.4 us  [exchange(): return lax.ppermute(shard, 'row', [(i, i ^ bits) for i in range(size)])]
    pallas_call x2 -> x1, Pallas kernels: 11 us -> 6.5 us  [conv_call(): pl.pallas_call(functools.partial(conv_kernel, span, group), grid_spec=plt...]
    unnamed x45 -> x56, local copies, waits for them, and re-layouts: 16.5 us -> 12.1 us
  transfers between devices with their start and end apart: 35 -> 27, of which waited for: 18 -> 7; matrix products, arithmetic and copies ran while one was open for 18% -> 4% of each run, Pallas kernels for 6% -> 46%
where the time goes in v2:
time: 269 us; the launch traced here: 267 us
  Pallas kernels  129 us (48%)
  waiting for transfers between devices  65.6 us (24%)
  starting transfers between devices  34.7 us (13%)
  local copies, waits for them, and re-layouts  14.5 us (5%)
  between operations  14.3 us (5%)
  other arithmetic  8.03 us (3%)
    pallas_call x6, Pallas kernels, product_call(): pl.pallas_call(functools.partial(product_kernel, len(pieces), (gradient,...  57.1 us
    ppermute x21, waiting for transfers between devices, exchange(): return lax.ppermute(shard, 'row', [(i, i ^ bits) for i in range(size)])  50.4 us
    ppermute x21, starting transfers between devices, exchange(): return lax.ppermute(shard, 'row', [(i, i ^ bits) for i in range(size)])  28.4 us
    pallas_call x2, Pallas kernels, weight_call(): pl.pallas_call(functools.partial(weight_kernel, len(grads), scale), grid=...  21.7 us
    pallas_call x4, Pallas kernels, take(): pl.pallas_call(copy_kernel, grid_spec=pltpu.PrefetchScalarGridSpec(num_sc...  13.5 us
    ppermute x3, waiting for transfers between devices, ring(): lax.ppermute(shard, 'col', [(i, (i + 1) % size) for i in range(size)])  12.6 us
    unnamed x56, local copies, waits for them, and re-layouts  12.1 us
    pallas_call x1, Pallas kernels, taps_call(): pl.pallas_call(functools.partial(taps_kernel, span, group), grid=(width /...  9.62 us
  transfers between devices with their start and end apart: 27, of which 7 were waited for; matrix products, arithmetic and copies ran while one was open for 4% of the time, Pallas kernels for 46%

profile of v2, /device:TPU:0, one launch (start us, length us, event | category | flops | bytes accessed | tf_op | source)
XLA Modules:
  0.0 266.6 jit_solution(17079408551387306667)
XLA Ops:
  7.7 1.9 multiply_convert_fusion.product_ref
  9.7 2.0 collective-permute-start
  12.7 2.6 collective-permute-done.rim_ref
  16.1 6.5 %conv.1 = (bf16[256,2048]{1,0:T(8,128)(2,1)}, f32[256,2048]{1,0:T(8,128)}) custom-call(s32[1]{0:T(128)} %bitcast.1.turn_ref, f32[128,256]{1,0:T(8,128)} %get-tuple-element.37.base_ref, bf16[128,2048]{1,0:T(8,128)(2,1)} %copy-done.26, bf16[256,2048]{1,0:T(8,128)(2,1)} %copy-done.12, bf16[256,2048]{1,0:T(8,128)(2,1)} %query_ref.3, ...), custom_call_target="tpu_custom_call" | custom-call | flops 2147483648 | bytes 6291456 | tf_op jit(solution)/shard_map/conv/pallas_call | solution.py:52
  22.6 7.5 %collective-permute-start.5 = (bf16[256,2048]{1,0:T(8,128)(2,1)S(1)}, bf16[256,2048]{1,0:T(8,128)(2,1)S(1)}, u32[]{:S(2)}, u32[]{:S(2)}) collective-permute-start(bf16[256,2048]{1,0:T(8,128)(2,1)S(1)} %copy-done.11), channel_id=1, source_target_pairs={{0,8},{4,12},{8,0},{12,4},{16,24},{20,28},{24,16},{28,20},{1,9},{5... | collective-permute-start | bytes 3145736 | tf_op jit(solution)/shard_map/ppermute | solution.py:217
  31.6 9.2 %product.6.refs_1_.refs_0_ = bf16[256,2048]{1,0:T(8,128)(2,1)} custom-call(bf16[256,2048]{1,0:T(8,128)(2,1)} %refs_4_.3, bf16[1024,2048]{1,0:T(8,128)(2,1)} %refs_2_.5, bf16[1024,2048]{1,0:T(8,128)(2,1)} %collective-permute-done.1.refs_0_.refs_2_.refs_3_, bf16[256,2048]{1,0:T(8,128)(2,1)} %get-tuple-element.21.refs_3_), custom_call_target="tpu_custom_call" | custom-call | flops 2147483648 | bytes 10485760 | tf_op jit(solution)/shard_map/product/pallas_call | solution.py:383
  40.8 12.0 %collective-permute-done.5.refs_0_ = bf16[256,2048]{1,0:T(8,128)(2,1)S(1)} collective-permute-done((bf16[256,2048]{1,0:T(8,128)(2,1)S(1)}, bf16[256,2048]{1,0:T(8,128)(2,1)S(1)}, u32[]{:S(2)}, u32[]{:S(2)}) %collective-permute-start.5) | collective-permute-done | bytes 1048608 | tf_op jit(solution)/shard_map/ppermute | solution.py:217
  59.0 9.1 %product.7.refs_3_ = bf16[256,2048]{1,0:T(8,128)(2,1)} custom-call(bf16[256,2048]{1,0:T(8,128)(2,1)} %once.6.refs_0_.refs_5_, bf16[1024,2048]{1,0:T(8,128)(2,1)} %refs_2_.5, bf16[1024,2048]{1,0:T(8,128)(2,1)} %collective-permute-done.1.refs_0_.refs_2_.refs_3_, bf16[128,2048]{1,0:T(8,128)(2,1)} %copy-done.15, bf16[128,2048]{1,0:T(8,128)(2,1)} %copy-done.16), custom_call_target="tpu_custom_call" | custom-call | flops 2147483648 | bytes 10485760 | tf_op jit(solution)/shard_map/product/pallas_call | solution.py:383
  69.8 9.1 %product.8.refs_4_ = bf16[256,2048]{1,0:T(8,128)(2,1)} custom-call(bf16[256,2048]{1,0:T(8,128)(2,1)} %once.7.refs_0_.refs_6_, bf16[1024,2048]{1,0:T(8,128)(2,1)} %refs_2_.5, bf16[1024,2048]{1,0:T(8,128)(2,1)} %collective-permute-done.1.refs_0_.refs_2_.refs_3_, bf16[256,2048]{1,0:T(8,128)(2,1)} %product.7.refs_3_), custom_call_target="tpu_custom_call" | custom-call | flops 2147483648 | bytes 10485760 | tf_op jit(solution)/shard_map/product/pallas_call | solution.py:383
  81.0 9.1 %product.9 = bf16[256,2048]{1,0:T(8,128)(2,1)} custom-call(bf16[128,2048]{1,0:T(8,128)(2,1)} %copy-done.13, bf16[128,2048]{1,0:T(8,128)(2,1)} %copy-done.14, bf16[1024,2048]{1,0:T(8,128)(2,1)} %refs_2_.5, bf16[1024,2048]{1,0:T(8,128)(2,1)} %collective-permute-done.1.refs_0_.refs_2_.refs_3_, bf16[256,2048]{1,0:T(8,128)(2,1)} %product.8.refs_4_), custom_call_target="tpu_custom_call" | custom-call | flops 2147483648 | bytes 10485760 | tf_op jit(solution)/shard_map/product/pallas_call | solution.py:383
  91.4 2.8 %collective-permute-done.7.refs_1_ = bf16[256,2048]{1,0:T(8,128)(2,1)S(1)} collective-permute-done((bf16[256,2048]{1,0:T(8,128)(2,1)}, bf16[256,2048]{1,0:T(8,128)(2,1)S(1)}, u32[]{:S(2)}, u32[]{:S(2)}) %collective-permute-start.7) | collective-permute-done | bytes 1048608 | tf_op jit(solution)/shard_map/ppermute | solution.py:217
  94.2 29.3 %collective-permute-done.8.refs_2_ = bf16[256,2048]{1,0:T(8,128)(2,1)S(1)} collective-permute-done((bf16[256,2048]{1,0:T(8,128)(2,1)}, bf16[256,2048]{1,0:T(8,128)(2,1)S(1)}, u32[]{:S(2)}, u32[]{:S(2)}) %collective-permute-start.8) | collective-permute-done | bytes 1048608 | tf_op jit(solution)/shard_map/ppermute | solution.py:217
  124.9 2.2 pick.1
  128.6 3.4 %take.6 = bf16[256,2048]{1,0:T(8,128)(2,1)} custom-call(s32[1]{0:T(128)} %bitcast.4.at_ref, bf16[4,256,2048]{2,1,0:T(8,128)(2,1)} %bitcast.10), custom_call_target="tpu_custom_call" | custom-call | bytes 2097152 | tf_op jit(solution)/shard_map/take/pallas_call | solution.py:276
  133.0 3.4 %take.7 = bf16[256,2048]{1,0:T(8,128)(2,1)} custom-call(s32[1]{0:T(128)} %bitcast.5.at_ref, bf16[4,256,2048]{2,1,0:T(8,128)(2,1)} %bitcast.11), custom_call_target="tpu_custom_call" | custom-call | bytes 2097152 | tf_op jit(solution)/shard_map/take/pallas_call | solution.py:276
  138.0 12.6 %collective-permute-done.12.refs_4_ = bf16[256,2048]{1,0:T(8,128)(2,1)S(1)} collective-permute-done((bf16[256,2048]{1,0:T(8,128)(2,1)}, bf16[256,2048]{1,0:T(8,128)(2,1)S(1)}, u32[]{:S(2)}, u32[]{:S(2)}) %collective-permute-start.12) | collective-permute-done | bytes 1048608 | tf_op jit(solution)/shard_map/ppermute | solution.py:222
  151.6 2.6 add.68.refs_4_
  154.3 3.4 %take.5.refs_0_ = bf16[256,2048]{1,0:T(8,128)(2,1)} custom-call(s32[1]{0:T(128)} %bitcast.3.at_ref, bf16[4,256,2048]{2,1,0:T(8,128)(2,1)} %bitcast.12), custom_call_target="tpu_custom_call" | custom-call | bytes 2097152 | tf_op jit(solution)/shard_map/take/pallas_call | solution.py:276
  159.6 2.2 collective-permute-start.4
  161.8 3.4 %take.4.refs_0_ = bf16[256,2048]{1,0:T(8,128)(2,1)} custom-call(s32[1]{0:T(128)} %bitcast.at_ref, bf16[4,256,2048]{2,1,0:T(8,128)(2,1)} %bitcast.13), custom_call_target="tpu_custom_call" | custom-call | bytes 2097152 | tf_op jit(solution)/shard_map/take/pallas_call | solution.py:276
  165.2 10.4 %product.10 = (bf16[256,2048]{1,0:T(8,128)(2,1)}, bf16[256,2048]{1,0:T(8,128)(2,1)}) custom-call(bf16[256,2048]{1,0:T(8,128)(2,1)} %copy-done.9, bf16[256,2048]{1,0:T(8,128)(2,1)} %copy-done.10, bf16[1024,2048]{1,0:T(8,128)(2,1)} %refs_2_.5, bf16[1024,2048]{1,0:T(8,128)(2,1)} %collective-permute-done.1.refs_0_.refs_2_.refs_3_, bf16[256,2048]{1,0:T(8,128)(2,1)} %add.68.refs_4_), custom_call_target="tpu_custom_call" | custom-call | flops 4294967296 | bytes 12582912 | tf_op jit(solution)/shard_map/product/pallas_call | solution.py:383
  177.3 2.6 add.69.refs_5_.refs_10_
  181.3 5.6 %collective-permute-done.4.refs_1_.refs_3_ = bf16[256,2048]{1,0:T(8,128)(2,1)S(1)} collective-permute-done((bf16[256,2048]{1,0:T(8,128)(2,1)}, bf16[256,2048]{1,0:T(8,128)(2,1)S(1)}, u32[]{:S(2)}, u32[]{:S(2)}) %collective-permute-start.4) | collective-permute-done | bytes 1048608 | tf_op jit(solution)/shard_map/ppermute | solution.py:217
  187.9 10.3 %product.11 = (bf16[256,2048]{1,0:T(8,128)(2,1)}, bf16[256,2048]{1,0:T(8,128)(2,1)}) custom-call(bf16[256,2048]{1,0:T(8,128)(2,1)} %take.4.refs_0_, bf16[256,2048]{1,0:T(8,128)(2,1)} %copy-done.17, bf16[1024,2048]{1,0:T(8,128)(2,1)} %refs_2_.5, bf16[1024,2048]{1,0:T(8,128)(2,1)} %collective-permute-done.1.refs_0_.refs_2_.refs_3_, ...), custom_call_target="tpu_custom_call" | custom-call | flops 4294967296 | bytes 12582912 | tf_op jit(solution)/shard_map/product/pallas_call | solution.py:383
  198.3 10.4 %weight.2 = (bf16[256,2048]{1,0:T(8,128)(2,1)}, bf16[256,2048]{1,0:T(8,128)(2,1)}, bf16[256,2048]{1,0:T(8,128)(2,1)}, bf16[256,2048]{1,0:T(8,128)(2,1)}) custom-call(bf16[256,2048]{1,0:T(8,128)(2,1)} %take.4.refs_0_, bf16[256,2048]{1,0:T(8,128)(2,1)} %copy-done.9, bf16[256,2048]{1,0:T(8,128)(2,1)} %copy-done.10, bf16[256,2048]{1,0:T(8,128)(2,1)} %copy-done.17, ...), custom_call_target="tpu_custom_call" | custom-call | flops 4294967296 | bytes 14680064 | tf_op jit(solution)/shard_map/weight/pallas_call | solution.py:436
  209.7 2.2 collective-permute-start.16
  212.0 2.6 add.70.grad_ref
  214.6 4.3 %gate.1 = (bf16[256,2048]{1,0:T(8,128)(2,1)}, bf16[256,2048]{1,0:T(8,128)(2,1)}, bf16[128,2048]{1,0:T(8,128)(2,1)}) custom-call(s32[1]{0:T(128)} %bitcast.1.turn_ref, bf16[256,2048]{1,0:T(8,128)(2,1)} %add.70.grad_ref, f32[256,2048]{1,0:T(8,128)} %get-tuple-element.27.conv_ref, bf16[256,2048]{1,0:T(8,128)(2,1)} %query_ref.3), custom_call_target="tpu_custom_call" | custom-call | flops 1048576 | bytes 6291456 | tf_op jit(solution)/shard_map/gate/pallas_call | solution.py:97
  220.2 9.6 %taps.1.refs_13_ = f32[128,128]{1,0:T(8,128)} custom-call(bf16[256,2048]{1,0:T(8,128)(2,1)} %get-tuple-element.29.grad_conv_ref, bf16[128,2048]{1,0:T(8,128)(2,1)} %copy-done.26, bf16[256,2048]{1,0:T(8,128)(2,1)} %copy-done.12), custom_call_target="tpu_custom_call" | custom-call | flops 4294967296 | bytes 2621440 | tf_op jit(solution)/shard_map/taps/pallas_call | solution.py:148
  231.0 11.3 %weight.3.refs_1_ = bf16[1024,2048]{1,0:T(8,128)(2,1)} custom-call(bf16[256,2048]{1,0:T(8,128)(2,1)} %take.4.refs_0_, bf16[256,2048]{1,0:T(8,128)(2,1)} %copy-done.9, bf16[256,2048]{1,0:T(8,128)(2,1)} %copy-done.10, bf16[256,2048]{1,0:T(8,128)(2,1)} %copy-done.17, bf16[256,2048]{1,0:T(8,128)(2,1)} %refs_4_.3, bf16[256,2048]{1,0:T(8,128)(2,1)} %once.6.refs_0_.refs_5_, ...), custom_call_target="tpu_custom_call" | custom-call | flops 4294967296 | bytes 14680064 | tf_op jit(solution)/shard_map/weight/pallas_call | solution.py:436
  246.5 6.7 %back.1 = (bf16[256,2048]{1,0:T(8,128)(2,1)}, bf16[256,2048]{1,0:T(8,128)(2,1)}) custom-call(f32[128,256]{1,0:T(8,128)} %get-tuple-element.36.base_ref, bf16[256,2048]{1,0:T(8,128)(2,1)} %get-tuple-element.29.grad_conv_ref, bf16[128,2048]{1,0:T(8,128)(2,1)} %copy-done.27, bf16[256,2048]{1,0:T(8,128)(2,1)} %key_ref.1, bf16[256,2048]{1,0:T(8,128)(2,1)} %value_ref.1, ...), custom_call_target="tpu_custom_call" | custom-call | flops 2147483648 | bytes 6291456 | tf_op jit(solution)/shard_map/back/pallas_call | solution.py:184
  255.5 2.9 %add_convert_fusion = bf16[256,2048]{1,0:T(8,128)(2,1)} fusion(bf16[256,2048]{1,0:T(8,128)(2,1)} %collective-permute-done.16, bf16[256,2048]{1,0:T(8,128)(2,1)S(1)} %copy-done.6, bf16[256,2048]{1,0:T(8,128)(2,1)S(1)} %copy-done.8, bf16[256,2048]{1,0:T(8,128)(2,1)S(1)} %copy-done.18), kind=kLoop, calls=%fused_computation | loop fusion | flops 4194304 | bytes 5242880 | tf_op jit(solution)/shard_map/convert_element_type | solution.py:496
  (118 shorter events, 39.2 us)
Async XLA Ops:
  7.2 121.4 %all-gather.3.cloned.1.call-start = ((), (), s32[]{:S(2)}) async-start(), calls=%async_computation | async-start | bytes 5242880 | tf_op jit(solution)/shard_map/all_gather | solution.py:467
  7.2 8.1 %collective-permute-start.1 = (bf16[1024,2048]{1,0:T(8,128)(2,1)}, bf16[1024,2048]{1,0:T(8,128)(2,1)}, u32[]{:S(2)}, u32[]{:S(2)}) collective-permute-start(bf16[1024,2048]{1,0:T(8,128)(2,1)} %refs_2_.5), channel_id=1, source_target_pairs={{0,4},{4,0},{8,12},{12,8},{16,20},{20,16},{24,28},{28,24},{1,5},{5... | collective-permute-start | bytes 12582920 | tf_op jit(solution)/shard_map/ppermute | solution.py:217
  9.7 5.5 %collective-permute-start = (bf16[128,2048]{1,0:T(8,128)(2,1)S(1)}, bf16[128,2048]{1,0:T(8,128)(2,1)S(1)}, u32[]{:S(2)}, u32[]{:S(2)}) collective-permute-start(bf16[128,2048]{1,0:T(8,128)(2,1)S(1)} %slice.12), channel_id=1, source_target_pairs={{0,4},{4,8},{8,12},{12,16},{16,20},{20,24},{24,28},{1,5},{5,9},{9,... | collective-permute-start | bytes 1572872 | tf_op jit(solution)/shard_map/ppermute | solution.py:212
  16.1 6.5 %copy-start.11 = (bf16[256,2048]{1,0:T(8,128)(2,1)S(1)}, bf16[256,2048]{1,0:T(8,128)(2,1)}, u32[]{:S(2)}) copy-start(bf16[256,2048]{1,0:T(8,128)(2,1)} %refs_4_.3) | copy-start | bytes 3145732
  22.6 30.2 %collective-permute-start.5 = (bf16[256,2048]{1,0:T(8,128)(2,1)S(1)}, bf16[256,2048]{1,0:T(8,128)(2,1)S(1)}, u32[]{:S(2)}, u32[]{:S(2)}) collective-permute-start(bf16[256,2048]{1,0:T(8,128)(2,1)S(1)} %copy-done.11), channel_id=1, source_target_pairs={{0,8},{4,12},{8,0},{12,4},{16,24},{20,28},{24,16},{28,20},{1,9},{5... | collective-permute-start | bytes 3145736 | tf_op jit(solution)/shard_map/ppermute | solution.py:217
  30.1 24.8 %collective-permute-start.6 = (bf16[256,2048]{1,0:T(8,128)(2,1)S(1)}, bf16[256,2048]{1,0:T(8,128)(2,1)S(1)}, u32[]{:S(2)}, u32[]{:S(2)}) collective-permute-start(bf16[256,2048]{1,0:T(8,128)(2,1)S(1)} %copy-done.11), channel_id=1, source_target_pairs={{0,16},{4,20},{8,24},{12,28},{16,0},{20,4},{24,8},{28,12},{1,17},{... | collective-permute-start | bytes 3145736 | tf_op jit(solution)/shard_map/ppermute | solution.py:217
  57.1 22.3 %collective-permute-start.9 = (bf16[128,2048]{1,0:T(8,128)(2,1)S(1)}, bf16[128,2048]{1,0:T(8,128)(2,1)S(1)}, u32[]{:S(2)}, u32[]{:S(2)}) collective-permute-start(bf16[128,2048]{1,0:T(8,128)(2,1)S(1)} %slice.13.refs_3_), channel_id=1, source_target_pairs={{0,16},{4,20},{8,24},{12,28},{16,0},{20,4},{24,8},{28,12},{1,17},{... | collective-permute-start | bytes 1572872 | tf_op jit(solution)/shard_map/ppermute | solution.py:217
  58.7 20.7 %collective-permute-start.10 = (bf16[128,2048]{1,0:T(8,128)(2,1)S(1)}, bf16[128,2048]{1,0:T(8,128)(2,1)S(1)}, u32[]{:S(2)}, u32[]{:S(2)}) collective-permute-start(bf16[128,2048]{1,0:T(8,128)(2,1)S(1)} %slice.14.refs_4_), channel_id=1, source_target_pairs={{0,8},{4,12},{8,0},{12,4},{16,24},{20,28},{24,16},{28,20},{1,9},{5... | collective-permute-start | bytes 1572872 | tf_op jit(solution)/shard_map/ppermute | solution.py:217
  68.1 26.1 %collective-permute-start.7 = (bf16[256,2048]{1,0:T(8,128)(2,1)}, bf16[256,2048]{1,0:T(8,128)(2,1)S(1)}, u32[]{:S(2)}, u32[]{:S(2)}) collective-permute-start(bf16[256,2048]{1,0:T(8,128)(2,1)} %product.7.refs_3_), channel_id=1, source_target_pairs={{0,8},{4,12},{8,0},{12,4},{16,24},{20,28},{24,16},{28,20},{1,9},{5... | collective-permute-start | bytes 3145736 | tf_op jit(solution)/shard_map/ppermute | solution.py:217
  78.9 44.6 %collective-permute-start.8 = (bf16[256,2048]{1,0:T(8,128)(2,1)}, bf16[256,2048]{1,0:T(8,128)(2,1)S(1)}, u32[]{:S(2)}, u32[]{:S(2)}) collective-permute-start(bf16[256,2048]{1,0:T(8,128)(2,1)} %product.8.refs_4_), channel_id=1, source_target_pairs={{0,16},{4,20},{8,24},{12,28},{16,0},{20,4},{24,8},{28,12},{1,17},{... | collective-permute-start | bytes 3145736 | tf_op jit(solution)/shard_map/ppermute | solution.py:217
  90.1 33.4 %collective-permute-start.11 = (bf16[256,2048]{1,0:T(8,128)(2,1)}, bf16[256,2048]{1,0:T(8,128)(2,1)S(1)}, u32[]{:S(2)}, u32[]{:S(2)}) collective-permute-start(bf16[256,2048]{1,0:T(8,128)(2,1)} %product.9), channel_id=1, source_target_pairs={{0,24},{4,28},{8,16},{12,20},{16,8},{20,12},{24,0},{28,4},{1,25},{... | collective-permute-start | bytes 3145736 | tf_op jit(solution)/shard_map/ppermute | solution.py:217
  94.2 29.4 %copy-start = (bf16[256,2048]{1,0:T(8,128)(2,1)}, bf16[256,2048]{1,0:T(8,128)(2,1)S(1)}, u32[]{:S(2)}) copy-start(bf16[256,2048]{1,0:T(8,128)(2,1)S(1)} %collective-permute-done.7.refs_1_) | copy-start | bytes 3145732
  127.1 23.5 %collective-permute-start.12 = (bf16[256,2048]{1,0:T(8,128)(2,1)}, bf16[256,2048]{1,0:T(8,128)(2,1)S(1)}, u32[]{:S(2)}, u32[]{:S(2)}) collective-permute-start(bf16[256,2048]{1,0:T(8,128)(2,1)} %pick.1), channel_id=1, source_target_pairs={{0,1},{1,2},{2,3},{3,0},{4,5},{5,6},{6,7},{7,4},{8,9},{9,10},{10,1... | collective-permute-start | bytes 3145736 | tf_op jit(solution)/shard_map/ppermute | solution.py:222
  131.9 25.7 %collective-permute-start.2 = (bf16[256,2048]{1,0:T(8,128)(2,1)}, bf16[256,2048]{1,0:T(8,128)(2,1)S(1)}, u32[]{:S(2)}, u32[]{:S(2)}) collective-permute-start(bf16[256,2048]{1,0:T(8,128)(2,1)} %take.6), channel_id=1, source_target_pairs={{0,8},{4,12},{8,0},{12,4},{16,24},{20,28},{24,16},{28,20},{1,9},{5... | collective-permute-start | bytes 3145736 | tf_op jit(solution)/shard_map/ppermute | solution.py:217
  136.3 21.3 %collective-permute-start.3 = (bf16[256,2048]{1,0:T(8,128)(2,1)}, bf16[256,2048]{1,0:T(8,128)(2,1)S(1)}, u32[]{:S(2)}, u32[]{:S(2)}) collective-permute-start(bf16[256,2048]{1,0:T(8,128)(2,1)} %take.7), channel_id=1, source_target_pairs={{0,16},{4,20},{8,24},{12,28},{16,0},{20,4},{24,8},{28,12},{1,17},{... | collective-permute-start | bytes 3145736 | tf_op jit(solution)/shard_map/ppermute | solution.py:217
  154.2 23.1 %collective-permute-start.13 = (bf16[256,2048]{1,0:T(8,128)(2,1)}, bf16[256,2048]{1,0:T(8,128)(2,1)}, u32[]{:S(2)}, u32[]{:S(2)}) collective-permute-start(bf16[256,2048]{1,0:T(8,128)(2,1)} %add.68.refs_4_), channel_id=1, source_target_pairs={{0,1},{1,2},{2,3},{3,0},{4,5},{5,6},{6,7},{7,4},{8,9},{9,10},{10,1... | collective-permute-start | bytes 3145736 | tf_op jit(solution)/shard_map/ppermute | solution.py:222
  159.6 27.2 %collective-permute-start.4 = (bf16[256,2048]{1,0:T(8,128)(2,1)}, bf16[256,2048]{1,0:T(8,128)(2,1)S(1)}, u32[]{:S(2)}, u32[]{:S(2)}) collective-permute-start(bf16[256,2048]{1,0:T(8,128)(2,1)} %once.5), channel_id=1, source_target_pairs={{0,24},{4,28},{8,16},{12,20},{16,8},{20,12},{24,0},{28,4},{1,25},{... | collective-permute-start | bytes 3145736 | tf_op jit(solution)/shard_map/ppermute | solution.py:217
  175.6 33.6 %collective-permute-start.15 = (bf16[256,2048]{1,0:T(8,128)(2,1)}, bf16[256,2048]{1,0:T(8,128)(2,1)S(1)}, u32[]{:S(2)}, u32[]{:S(2)}) collective-permute-start(bf16[256,2048]{1,0:T(8,128)(2,1)} %get-tuple-element.24), channel_id=1, source_target_pairs={{0,16},{4,20},{8,24},{12,28},{16,0},{20,4},{24,8},{28,12},{1,17},{... | collective-permute-start | bytes 3145736 | tf_op jit(solution)/shard_map/ppermute | solution.py:217
  176.0 33.3 %collective-permute-start.14 = (bf16[256,2048]{1,0:T(8,128)(2,1)}, bf16[256,2048]{1,0:T(8,128)(2,1)S(1)}, u32[]{:S(2)}, u32[]{:S(2)}) collective-permute-start(bf16[256,2048]{1,0:T(8,128)(2,1)} %get-tuple-element.22.refs_5_.refs_4_), channel_id=1, source_target_pairs={{0,8},{4,12},{8,0},{12,4},{16,24},{20,28},{24,16},{28,20},{1,9},{5... | collective-permute-start | bytes 3145736 | tf_op jit(solution)/shard_map/ppermute | solution.py:217
  179.9 29.8 %collective-permute-start.17 = (bf16[256,2048]{1,0:T(8,128)(2,1)}, bf16[256,2048]{1,0:T(8,128)(2,1)}, u32[]{:S(2)}, u32[]{:S(2)}) collective-permute-start(bf16[256,2048]{1,0:T(8,128)(2,1)} %add.69.refs_5_.refs_10_), channel_id=1, source_target_pairs={{0,1},{1,2},{2,3},{3,0},{4,5},{5,6},{6,7},{7,4},{8,9},{9,10},{10,1... | collective-permute-start | bytes 3145736 | tf_op jit(solution)/shard_map/ppermute | solution.py:222
  208.7 10.2 %collective-permute-start.20 = (bf16[256,2048]{1,0:T(8,128)(2,1)}, bf16[256,2048]{1,0:T(8,128)(2,1)S(1)}, u32[]{:S(2)}, u32[]{:S(2)}) collective-permute-start(bf16[256,2048]{1,0:T(8,128)(2,1)} %get-tuple-element.26.refs_5_), channel_id=1, source_target_pairs={{0,4},{4,0},{8,12},{12,8},{16,20},{20,16},{24,28},{28,24},{1,5},{5... | collective-permute-start | bytes 3145736 | tf_op jit(solution)/shard_map/ppermute | solution.py:217
  208.7 21.1 %collective-permute-start.21 = (bf16[256,2048]{1,0:T(8,128)(2,1)}, bf16[256,2048]{1,0:T(8,128)(2,1)}, u32[]{:S(2)}, u32[]{:S(2)}) collective-permute-start(bf16[256,2048]{1,0:T(8,128)(2,1)} %get-tuple-element.31), channel_id=1, source_target_pairs={{0,4},{4,0},{8,12},{12,8},{16,20},{20,16},{24,28},{28,24},{1,5},{5... | collective-permute-start | bytes 3145736 | tf_op jit(solution)/shard_map/ppermute | solution.py:217
  209.2 21.8 %collective-permute-start.22 = (bf16[256,2048]{1,0:T(8,128)(2,1)}, bf16[256,2048]{1,0:T(8,128)(2,1)}, u32[]{:S(2)}, u32[]{:S(2)}) collective-permute-start(bf16[256,2048]{1,0:T(8,128)(2,1)} %get-tuple-element.32), channel_id=1, source_target_pairs={{0,4},{4,0},{8,12},{12,8},{16,20},{20,16},{24,28},{28,24},{1,5},{5... | collective-permute-start | bytes 3145736 | tf_op jit(solution)/shard_map/ppermute | solution.py:217
  209.3 21.7 %collective-permute-start.23 = (bf16[256,2048]{1,0:T(8,128)(2,1)}, bf16[256,2048]{1,0:T(8,128)(2,1)}, u32[]{:S(2)}, u32[]{:S(2)}) collective-permute-start(bf16[256,2048]{1,0:T(8,128)(2,1)} %get-tuple-element.33), channel_id=1, source_target_pairs={{0,4},{4,0},{8,12},{12,8},{16,20},{20,16},{24,28},{28,24},{1,5},{5... | collective-permute-start | bytes 3145736 | tf_op jit(solution)/shard_map/ppermute | solution.py:217
  209.7 45.7 %collective-permute-start.16 = (bf16[256,2048]{1,0:T(8,128)(2,1)}, bf16[256,2048]{1,0:T(8,128)(2,1)}, u32[]{:S(2)}, u32[]{:S(2)}) collective-permute-start(bf16[256,2048]{1,0:T(8,128)(2,1)} %get-tuple-element.25), channel_id=1, source_target_pairs={{0,24},{4,28},{8,16},{12,20},{16,8},{20,12},{24,0},{28,4},{1,25},{... | collective-permute-start | bytes 3145736 | tf_op jit(solution)/shard_map/ppermute | solution.py:217
  218.9 10.9 %copy-start.19 = (bf16[256,2048]{1,0:T(8,128)(2,1)}, bf16[256,2048]{1,0:T(8,128)(2,1)S(1)}, u32[]{:S(2)}) copy-start(bf16[256,2048]{1,0:T(8,128)(2,1)S(1)} %collective-permute-done.20.refs_9_) | copy-start | bytes 3145732
  218.9 26.8 %collective-permute-start.18 = (bf16[128,2048]{1,0:T(8,128)(2,1)}, bf16[128,2048]{1,0:T(8,128)(2,1)S(1)}, u32[]{:S(2)}, u32[]{:S(2)}) collective-permute-start(bf16[128,2048]{1,0:T(8,128)(2,1)} %get-tuple-element.30), channel_id=1, source_target_pairs={{4,0},{8,4},{12,8},{16,12},{20,16},{24,20},{28,24},{5,1},{9,5},{13... | collective-permute-start | bytes 1572872 | tf_op jit(solution)/shard_map/ppermute | solution.py:212
  229.8 12.5 %collective-permute-start.19 = (f32[128,128]{1,0:T(8,128)}, f32[128,128]{1,0:T(8,128)S(1)}, u32[]{:S(2)}, u32[]{:S(2)}) collective-permute-start(f32[128,128]{1,0:T(8,128)} %taps.1.refs_13_), channel_id=1, source_target_pairs={{0,4},{4,0},{8,12},{12,8},{16,20},{20,16},{24,28},{28,24},{1,5},{5... | collective-permute-start | bytes 196616 | tf_op jit(solution)/shard_map/ppermute | solution.py:217
  244.0 9.2 %collective-permute-start.24 = (f32[128,128]{1,0:T(8,128)S(1)}, f32[128,128]{1,0:T(8,128)S(1)}, u32[]{:S(2)}, u32[]{:S(2)}) collective-permute-start(f32[128,128]{1,0:T(8,128)S(1)} %add.62.refs_0_), channel_id=1, source_target_pairs={{0,8},{4,12},{8,0},{12,4},{16,24},{20,28},{24,16},{28,20},{1,9},{5... | collective-permute-start | bytes 196616 | tf_op jit(solution)/shard_map/ppermute | solution.py:217
  246.5 9.0 %copy-start.8 = (bf16[256,2048]{1,0:T(8,128)(2,1)S(1)}, bf16[256,2048]{1,0:T(8,128)(2,1)}, u32[]{:S(2)}) copy-start(bf16[256,2048]{1,0:T(8,128)(2,1)} %copy-done.7) | copy-start | bytes 3145732
  246.5 9.0 %copy-start.18 = (bf16[256,2048]{1,0:T(8,128)(2,1)S(1)}, bf16[256,2048]{1,0:T(8,128)(2,1)}, u32[]{:S(2)}) copy-start(bf16[256,2048]{1,0:T(8,128)(2,1)} %get-tuple-element.23.refs_9_) | copy-start | bytes 3145732
  254.7 4.3 %collective-permute-start.25 = (f32[128,128]{1,0:T(8,128)S(1)}, f32[128,128]{1,0:T(8,128)S(1)}, u32[]{:S(2)}, u32[]{:S(2)}) collective-permute-start(f32[128,128]{1,0:T(8,128)S(1)} %add.63), channel_id=1, source_target_pairs={{0,16},{4,20},{8,24},{12,28},{16,0},{20,4},{24,8},{28,12},{1,17},{... | collective-permute-start | bytes 196616 | tf_op jit(solution)/shard_map/ppermute | solution.py:217
  (23 other events, 39.4 us)
Sparse Core Ops, SparseCore 0:
  22.7 87.9 all-gather.2

commit v3 on v2

--- a/solution.py
+++ b/solution.py
@@ -70,11 +70,6 @@
             jax.ShapeDtypeStruct((tokens, width), bf16),
             jax.ShapeDtypeStruct((tokens, width), f32),
         ],
-        cost_estimate=pl.CostEstimate(
-            flops=4 * span * tokens * width * LANES // group,
-            bytes_accessed=12 * tokens * width,
-            transcendentals=0,
-        ),
         name="conv",
     )(turn, base, rim, product, query, *after)
 
@@ -111,7 +106,6 @@
             jax.ShapeDtypeStruct((tokens, width), bf16),
             jax.ShapeDtypeStruct((span, width), bf16),
         ],
-        cost_estimate=pl.CostEstimate(flops=2 * tokens * width, bytes_accessed=12 * tokens * width, transcendentals=0),
         name="gate",
     )(turn, grad, conv, query)
 
@@ -151,11 +145,6 @@
         in_specs=[block(tokens), block(span), block(tokens)] + [pl.BlockSpec(memory_space=pl.ANY)] * len(after),
         out_specs=pl.BlockSpec((lanes // group, span), lambda i: (i, 0)),
         out_shape=jax.ShapeDtypeStruct((width // group, span), f32),
-        cost_estimate=pl.CostEstimate(
-            flops=8 * span * tokens * width * LANES // group,
-            bytes_accessed=5 * tokens * width,
-            transcendentals=0,
-        ),
         name="taps",
     )(grad_conv, rim, product, *after)
 
@@ -197,11 +186,6 @@
             jax.ShapeDtypeStruct((tokens, width), bf16),
             jax.ShapeDtypeStruct((tokens, width), bf16),
         ],
-        cost_estimate=pl.CostEstimate(
-            flops=4 * span * tokens * width * LANES // group,
-            bytes_accessed=12 * tokens * width,
-            transcendentals=0,
-        ),
         name="back",
     )(base, grad_conv, rim, key, value, *after)
 
@@ -261,30 +245,8 @@
         in_specs=[pl.BlockSpec(memory_space=pltpu.SMEM)] + [pl.BlockSpec(memory_space=pl.ANY)] * 4,
         out_specs=pl.BlockSpec(memory_space=pltpu.VMEM),
         out_shape=jax.ShapeDtypeStruct(pieces[0].shape, pieces[0].dtype),
-        cost_estimate=pl.CostEstimate(flops=0, bytes_accessed=4 * pieces[0].size, transcendentals=0),
         name="pick",
     )(at.astype(jnp.int32).reshape(1), *pieces)
-
-
-def copy_kernel(at_ref, in_ref, out_ref):
-    out_ref[...] = in_ref[0]
-
-
-def take(stack, at):
-    _, rows, columns = stack.shape
-    part = rows // 4
-    return pl.pallas_call(
-        copy_kernel,
-        grid_spec=pltpu.PrefetchScalarGridSpec(
-            num_scalar_prefetch=1,
-            grid=(4,),
-            in_specs=[pl.BlockSpec((1, part, columns), lambda i, at: (at[0], i, 0))],
-            out_specs=pl.BlockSpec((part, columns), lambda i, at: (i, 0)),
-        ),
-        out_shape=jax.ShapeDtypeStruct((rows, columns), stack.dtype),
-        cost_estimate=pl.CostEstimate(flops=0, bytes_accessed=4 * rows * columns, transcendentals=0),
-        name="take",
-    )(at.astype(jnp.int32).reshape(1), stack)
 
 
 def add_kernel(parts, at_ref, *refs):
@@ -325,7 +287,6 @@
             pltpu.VMEM(came.shape, bf16),
             pltpu.SemaphoreType.DMA((2, parts)),
         ],
-        cost_estimate=pl.CostEstimate(flops=came.size, bytes_accessed=6 * came.size, transcendentals=0),
         name="add",
     )(at.astype(jnp.int32).reshape(1), *pieces, came, *after)
 
@@ -366,7 +327,7 @@
 
 
 def product_call(pieces, own, other, after, outs, gradient):
-    block = 256
+    block = 512
     rows = sum(piece.shape[0] for piece in pieces)
     depth = pieces[0].shape[1]
     if gradient:
@@ -390,11 +351,6 @@
             out_shape=[jax.ShapeDtypeStruct((rows // outs, columns), bf16)] * outs,
             scratch_shapes=[pltpu.VMEM((rows, depth), bf16)],
             compiler_params=pltpu.CompilerParams(vmem_limit_bytes=GRANT),
-            cost_estimate=pl.CostEstimate(
-                flops=2 * rows * depth * columns,
-                bytes_accessed=2 * (rows * depth + depth * columns + rows * columns),
-                transcendentals=0,
-            ),
             name="product",
         )(*pieces, own, other, *after)
     )
@@ -448,11 +404,6 @@
         else [jax.ShapeDtypeStruct((block, columns), bf16)] * 4,
         scratch_shapes=[pltpu.VMEM((rows, columns), bf16)],
         compiler_params=pltpu.CompilerParams(vmem_limit_bytes=GRANT),
-        cost_estimate=pl.CostEstimate(
-            flops=2 * rows * width * columns,
-            bytes_accessed=2 * rows * (width + columns) + 4 * width * columns,
-            transcendentals=0,
-        ),
         name="weight",
     )(*held, *grads, *came, *after)
 
@@ -464,7 +415,6 @@
     half, part = out_weight.shape[0], tokens // 2
     weights = (out_weight, other_weight)
 
-    panel = lax.all_gather(gated, "col")
     kept = product_call([out_grad], *weights, [gated], 1, True)[0]
     grad_x, grad_y = [once(piece, kept) for piece in neighbours]
     far_x, far_y = grad_x[:part], grad_y[part:]
@@ -472,17 +422,21 @@
     grads = [out_grad, grad_x, grad_y, *far]
 
     to_x = product_call([grad_x], *weights, [far_x, far_y], 1, True)[0]
-    to_y = product_call([grad_y], *weights, [to_x], 1, True)[0]
+    z1 = once(ring(gated), to_x)
+    z2 = ring(z1)
+    to_y = product_call([grad_y], *weights, [z1], 1, True)[0]
     to_far = product_call(far, *weights, [to_y], 1, True)[0]
-    back_x, back_y = exchange(to_x, 2), exchange(to_y, 4)
-    partial = [kept, back_x, back_y, exchange(to_far, 6)]
+    z2 = once(z2, to_far)
+    z3 = ring(z2)
+    partial = [kept, exchange(to_x, 2), exchange(to_y, 4), exchange(to_far, 6)]
 
     def add(step, total, *after):
         return pick_and_add(partial, chip ^ (plane + 7 - step) % 4, ring(total), after)
 
     first = add(1, pick(partial, chip ^ (plane + 3) % 4))
 
-    held = [take(panel, chip ^ d) for d in range(4)]
+    pieces = [gated, z1, z2, z3]
+    held = [pick(pieces, (plane + 4 - (chip ^ d)) % 4) for d in range(4)]
     held_x, held_y = exchange(held[1], 2), exchange(held[2], 4)
     held_far = exchange(once(held[3], held_x, held_y), 6)
     near = product_call([held_x, held_y], *weights, [first], 2, False)

time: 269 us -> 250 us (0.929)
  Pallas kernels: 129 us -> 114 us
  between operations: 14.3 us -> 0.85 us
  waiting for transfers between devices: 65.6 us -> 72.3 us
    pallas_call x4 -> x0, Pallas kernels: 13.5 us -> none  [take(): pl.pallas_call(copy_kernel, grid_spec=pltpu.PrefetchScalarGridSpec(num_sc...]
    ppermute x3 -> x6, waiting for transfers between devices: 12.6 us -> 23.6 us  [ring(): lax.ppermute(shard, 'col', [(i, (i + 1) % size) for i in range(size)])]
    pallas_call x6, Pallas kernels: 57.1 us -> 46.3 us  [product_call(): pl.pallas_call(functools.partial(product_kernel, len(pieces), (gradient,...]
    pallas_call x1 -> x5, Pallas kernels: 2.19 us -> 11.2 us  [pick(): pl.pallas_call(pick_kernel, in_specs=[pl.BlockSpec(memory_space=pltpu.SME...]
    ppermute x3 -> x6, starting transfers between devices: 2.93 us -> 6.57 us  [ring(): lax.ppermute(shard, 'col', [(i, (i + 1) % size) for i in range(size)])]
    unnamed x56 -> x52, local copies, waits for them, and re-layouts: 12.1 us -> 12 us
  transfers between devices with their start and end apart: 27 -> 29, of which waited for: 7 -> 10; matrix products, arithmetic and copies ran while one was open for 4% -> 5% of each run, Pallas kernels for 46% -> 46%
where the time goes in v3:
time: 250 us; the launch traced here: 249 us
  Pallas kernels  114 us (46%)
  waiting for transfers between devices  72.3 us (29%)
  starting transfers between devices  36.7 us (15%)
  local copies, waits for them, and re-layouts  16.9 us (7%)
  other arithmetic  8.03 us (3%)
    ppermute x21, waiting for transfers between devices, exchange(): return lax.ppermute(shard, 'row', [(i, i ^ bits) for i in range(size)])  48.7 us
    pallas_call x6, Pallas kernels, product_call(): pl.pallas_call(functools.partial(product_kernel, len(pieces), (gradient,...  46.3 us
    ppermute x21, starting transfers between devices, exchange(): return lax.ppermute(shard, 'row', [(i, i ^ bits) for i in range(size)])  26.1 us
    ppermute x6, waiting for transfers between devices, ring(): lax.ppermute(shard, 'col', [(i, (i + 1) % size) for i in range(size)])  23.6 us
    pallas_call x2, Pallas kernels, weight_call(): pl.pallas_call(functools.partial(weight_kernel, len(grads), scale), grid=...  21.7 us
    unnamed x52, local copies, waits for them, and re-layouts  12 us
    pallas_call x5, Pallas kernels, pick(): pl.pallas_call(pick_kernel, in_specs=[pl.BlockSpec(memory_space=pltpu.SME...  11.2 us
    pallas_call x1, Pallas kernels, taps_call(): pl.pallas_call(functools.partial(taps_kernel, span, group), grid=(width /...  9.62 us
  transfers between devices with their start and end apart: 29, of which 10 were waited for; matrix products, arithmetic and copies ran while one was open for 5% of the time, Pallas kernels for 46%

profile of v3, /device:TPU:0, one launch (start us, length us, event | category | flops | bytes accessed | tf_op | source)
XLA Modules:
  0.0 249.1 jit_solution(17836268142985790540)
XLA Ops:
  4.0 2.8 %collective-permute-start = (bf16[128,2048]{1,0:T(8,128)(2,1)}, bf16[128,2048]{1,0:T(8,128)(2,1)}, u32[]{:S(2)}, u32[]{:S(2)}) collective-permute-start(bf16[128,2048]{1,0:T(8,128)(2,1)} %slice.12), channel_id=1, source_target_pairs={{0,4},{4,8},{8,12},{12,16},{16,20},{20,24},{24,28},{1,5},{5,9},{9,... | collective-permute-start | bytes 1572872 | tf_op jit(solution)/shard_map/ppermute | solution.py:196
  6.7 2.2 collective-permute-start.3
  11.4 6.4 %conv.1 = (bf16[256,2048]{1,0:T(8,128)(2,1)}, f32[256,2048]{1,0:T(8,128)}) custom-call(s32[1]{0:T(128)} %bitcast.1.turn_ref, f32[128,256]{1,0:T(8,128)} %get-tuple-element.37.base_ref, bf16[128,2048]{1,0:T(8,128)(2,1)} %collective-permute-done.rim_ref, bf16[256,2048]{1,0:T(8,128)(2,1)} %copy-done.9, bf16[256,2048]{1,0:T(8,128)(2,1)} %query_ref.3, ...), custom_call_target="tpu_custom_call" | custom-call | tf_op jit(solution)/shard_map/conv/pallas_call | solution.py:52
  19.4 7.3 %product.6.refs_1_.refs_0_ = bf16[256,2048]{1,0:T(8,128)(2,1)} custom-call(bf16[256,2048]{1,0:T(8,128)(2,1)} %refs_4_.3, bf16[1024,2048]{1,0:T(8,128)(2,1)} %refs_2_.5, bf16[1024,2048]{1,0:T(8,128)(2,1)} %collective-permute-done.1.refs_0_.refs_2_.refs_3_, bf16[256,2048]{1,0:T(8,128)(2,1)} %get-tuple-element.21.refs_3_.refs_0_), custom_call_target="tpu_custom_call" | custom-call | tf_op jit(solution)/shard_map/product/pallas_call | solution.py:344
  26.7 6.1 %collective-permute-done.3.refs_0_ = bf16[256,2048]{1,0:T(8,128)(2,1)S(1)} collective-permute-done((bf16[256,2048]{1,0:T(8,128)(2,1)}, bf16[256,2048]{1,0:T(8,128)(2,1)S(1)}, u32[]{:S(2)}, u32[]{:S(2)}) %collective-permute-start.3) | collective-permute-done | bytes 1048608 | tf_op jit(solution)/shard_map/ppermute | solution.py:201
  35.7 2.7 %collective-permute-done.4.refs_0_ = bf16[256,2048]{1,0:T(8,128)(2,1)S(1)} collective-permute-done((bf16[256,2048]{1,0:T(8,128)(2,1)}, bf16[256,2048]{1,0:T(8,128)(2,1)S(1)}, u32[]{:S(2)}, u32[]{:S(2)}) %collective-permute-start.4) | collective-permute-done | bytes 1048608 | tf_op jit(solution)/shard_map/ppermute | solution.py:201
  41.4 7.3 %product.7.refs_1_ = bf16[256,2048]{1,0:T(8,128)(2,1)} custom-call(bf16[256,2048]{1,0:T(8,128)(2,1)} %once.7.refs_0_.refs_5_, bf16[1024,2048]{1,0:T(8,128)(2,1)} %refs_2_.5, bf16[1024,2048]{1,0:T(8,128)(2,1)} %collective-permute-done.1.refs_0_.refs_2_.refs_3_, bf16[128,2048]{1,0:T(8,128)(2,1)} %slice.13.refs_3_, bf16[128,2048]{1,0:T(8,128)(2,1)} %slice.14.refs_4_), custom_call_target="tpu_custom_call" | custom-call | tf_op jit(solution)/shard_map/product/pallas_call | solution.py:344
  50.9 4.5 %collective-permute-start.6 = (bf16[128,2048]{1,0:T(8,128)(2,1)}, bf16[128,2048]{1,0:T(8,128)(2,1)S(1)}, u32[]{:S(2)}, u32[]{:S(2)}) collective-permute-start(bf16[128,2048]{1,0:T(8,128)(2,1)} %slice.13.refs_3_), channel_id=1, source_target_pairs={{0,16},{4,20},{8,24},{12,28},{16,0},{20,4},{24,8},{28,12},{1,17},{... | collective-permute-start | bytes 1572872 | tf_op jit(solution)/shard_map/ppermute | solution.py:201
  57.5 7.3 %product.8.refs_4_ = bf16[256,2048]{1,0:T(8,128)(2,1)} custom-call(bf16[256,2048]{1,0:T(8,128)(2,1)} %once.8.refs_0_.refs_6_, bf16[1024,2048]{1,0:T(8,128)(2,1)} %refs_2_.5, bf16[1024,2048]{1,0:T(8,128)(2,1)} %collective-permute-done.1.refs_0_.refs_2_.refs_3_, bf16[256,2048]{1,0:T(8,128)(2,1)} %once.9.refs_3_.refs_1_), custom_call_target="tpu_custom_call" | custom-call | tf_op jit(solution)/shard_map/product/pallas_call | solution.py:344
  65.9 2.6 %collective-permute-done.6.refs_0_.refs_7_ = bf16[128,2048]{1,0:T(8,128)(2,1)S(1)} collective-permute-done((bf16[128,2048]{1,0:T(8,128)(2,1)}, bf16[128,2048]{1,0:T(8,128)(2,1)S(1)}, u32[]{:S(2)}, u32[]{:S(2)}) %collective-permute-start.6) | collective-permute-done | bytes 524320 | tf_op jit(solution)/shard_map/ppermute | solution.py:201
  71.4 7.2 %product.9.refs_1_ = bf16[256,2048]{1,0:T(8,128)(2,1)} custom-call(bf16[128,2048]{1,0:T(8,128)(2,1)} %copy-done.11, bf16[128,2048]{1,0:T(8,128)(2,1)} %copy-done.12, bf16[1024,2048]{1,0:T(8,128)(2,1)} %refs_2_.5, bf16[1024,2048]{1,0:T(8,128)(2,1)} %collective-permute-done.1.refs_0_.refs_2_.refs_3_, bf16[256,2048]{1,0:T(8,128)(2,1)} %product.8.refs_4_), custom_call_target="tpu_custom_call" | custom-call | tf_op jit(solution)/shard_map/product/pallas_call | solution.py:344
  78.6 2.5 %collective-permute-start.14 = (bf16[256,2048]{1,0:T(8,128)(2,1)}, bf16[256,2048]{1,0:T(8,128)(2,1)}, u32[]{:S(2)}, u32[]{:S(2)}) collective-permute-start(bf16[256,2048]{1,0:T(8,128)(2,1)} %product.9.refs_1_), channel_id=1, source_target_pairs={{0,24},{4,28},{8,16},{12,20},{16,8},{20,12},{24,0},{28,4},{1,25},{... | collective-permute-start | bytes 3145736 | tf_op jit(solution)/shard_map/ppermute | solution.py:201
  82.6 10.4 %collective-permute-done.12.refs_1_ = bf16[256,2048]{1,0:T(8,128)(2,1)S(1)} collective-permute-done((bf16[256,2048]{1,0:T(8,128)(2,1)}, bf16[256,2048]{1,0:T(8,128)(2,1)S(1)}, u32[]{:S(2)}, u32[]{:S(2)}) %collective-permute-start.12) | collective-permute-done | bytes 1048608 | tf_op jit(solution)/shard_map/ppermute | solution.py:201
  93.0 21.5 %collective-permute-done.14.refs_3_ = bf16[256,2048]{1,0:T(8,128)(2,1)} collective-permute-done((bf16[256,2048]{1,0:T(8,128)(2,1)}, bf16[256,2048]{1,0:T(8,128)(2,1)}, u32[]{:S(2)}, u32[]{:S(2)}) %collective-permute-start.14) | collective-permute-done | bytes 1048608 | tf_op jit(solution)/shard_map/ppermute | solution.py:201
  114.5 2.3 pick.9
  119.3 2.3 pick.7
  122.5 2.2 pick.8
  126.2 16.3 %collective-permute-done.15.refs_4_ = bf16[256,2048]{1,0:T(8,128)(2,1)S(1)} collective-permute-done((bf16[256,2048]{1,0:T(8,128)(2,1)}, bf16[256,2048]{1,0:T(8,128)(2,1)S(1)}, u32[]{:S(2)}, u32[]{:S(2)}) %collective-permute-start.15) | collective-permute-done | bytes 1048608 | tf_op jit(solution)/shard_map/ppermute | solution.py:206
  143.4 2.7 %add.91.refs_4_ = bf16[256,2048]{1,0:T(8,128)(2,1)} custom-call(s32[1]{0:T(128)} %bitcast.5.at_ref, bf16[256,2048]{1,0:T(8,128)(2,1)} %product.6.refs_1_.refs_0_, bf16[256,2048]{1,0:T(8,128)(2,1)} %copy-done.4, bf16[256,2048]{1,0:T(8,128)(2,1)} %copy-done.5, bf16[256,2048]{1,0:T(8,128)(2,1)} %collective-permute-done.14.refs_3_, bf16[256,2048]{1,0:T(8,128)(2,1)} %copy-done.19), custom_call_target="tpu_custom_call" | custom-call | tf_op jit(solution)/shard_map/add/pallas_call | solution.py:280
  147.2 2.3 pick.6.refs_0_
  153.5 8.6 %product.10 = (bf16[256,2048]{1,0:T(8,128)(2,1)}, bf16[256,2048]{1,0:T(8,128)(2,1)}) custom-call(bf16[256,2048]{1,0:T(8,128)(2,1)} %copy-done.6, bf16[256,2048]{1,0:T(8,128)(2,1)} %copy-done.7, bf16[1024,2048]{1,0:T(8,128)(2,1)} %refs_2_.5, bf16[1024,2048]{1,0:T(8,128)(2,1)} %collective-permute-done.1.refs_0_.refs_2_.refs_3_, bf16[256,2048]{1,0:T(8,128)(2,1)} %add.91.refs_4_), custom_call_target="tpu_custom_call" | custom-call | tf_op jit(solution)/shard_map/product/pallas_call | solution.py:344
  163.6 7.4 %collective-permute-done.16.refs_4_ = bf16[256,2048]{1,0:T(8,128)(2,1)} collective-permute-done((bf16[256,2048]{1,0:T(8,128)(2,1)}, bf16[256,2048]{1,0:T(8,128)(2,1)}, u32[]{:S(2)}, u32[]{:S(2)}) %collective-permute-start.16) | collective-permute-done | bytes 1048608 | tf_op jit(solution)/shard_map/ppermute | solution.py:206
  171.0 2.6 %add.92.refs_5_.refs_10_ = bf16[256,2048]{1,0:T(8,128)(2,1)} custom-call(s32[1]{0:T(128)} %bitcast.7.at_ref, bf16[256,2048]{1,0:T(8,128)(2,1)} %product.6.refs_1_.refs_0_, bf16[256,2048]{1,0:T(8,128)(2,1)} %copy-done.4, bf16[256,2048]{1,0:T(8,128)(2,1)} %copy-done.5, bf16[256,2048]{1,0:T(8,128)(2,1)} %collective-permute-done.14.refs_3_, ...), custom_call_target="tpu_custom_call" | custom-call | tf_op jit(solution)/shard_map/add/pallas_call | solution.py:280
  176.5 2.3 collective-permute-done.11.refs_1_.refs_3_
  179.7 8.6 %product.11 = (bf16[256,2048]{1,0:T(8,128)(2,1)}, bf16[256,2048]{1,0:T(8,128)(2,1)}) custom-call(bf16[256,2048]{1,0:T(8,128)(2,1)} %pick.5.refs_0_, bf16[256,2048]{1,0:T(8,128)(2,1)} %copy-done.10, bf16[1024,2048]{1,0:T(8,128)(2,1)} %refs_2_.5, bf16[1024,2048]{1,0:T(8,128)(2,1)} %collective-permute-done.1.refs_0_.refs_2_.refs_3_, ...), custom_call_target="tpu_custom_call" | custom-call | tf_op jit(solution)/shard_map/product/pallas_call | solution.py:344
  188.4 10.4 %weight.2 = (bf16[256,2048]{1,0:T(8,128)(2,1)}, bf16[256,2048]{1,0:T(8,128)(2,1)}, bf16[256,2048]{1,0:T(8,128)(2,1)}, bf16[256,2048]{1,0:T(8,128)(2,1)}) custom-call(bf16[256,2048]{1,0:T(8,128)(2,1)} %pick.5.refs_0_, bf16[256,2048]{1,0:T(8,128)(2,1)} %copy-done.6, bf16[256,2048]{1,0:T(8,128)(2,1)} %copy-done.7, bf16[256,2048]{1,0:T(8,128)(2,1)} %copy-done.10, ...), custom_call_target="tpu_custom_call" | custom-call | tf_op jit(solution)/shard_map/weight/pallas_call | solution.py:392
  201.9 2.7 %add.93.grad_ref = bf16[256,2048]{1,0:T(8,128)(2,1)} custom-call(s32[1]{0:T(128)} %bitcast.8.at_ref, bf16[256,2048]{1,0:T(8,128)(2,1)} %product.6.refs_1_.refs_0_, bf16[256,2048]{1,0:T(8,128)(2,1)} %copy-done.4, bf16[256,2048]{1,0:T(8,128)(2,1)} %copy-done.5, bf16[256,2048]{1,0:T(8,128)(2,1)} %collective-permute-done.14.refs_3_, ...), custom_call_target="tpu_custom_call" | custom-call | tf_op jit(solution)/shard_map/add/pallas_call | solution.py:280
  204.6 4.3 %gate.1 = (bf16[256,2048]{1,0:T(8,128)(2,1)}, bf16[256,2048]{1,0:T(8,128)(2,1)}, bf16[128,2048]{1,0:T(8,128)(2,1)}) custom-call(s32[1]{0:T(128)} %bitcast.1.turn_ref, bf16[256,2048]{1,0:T(8,128)(2,1)} %add.93.grad_ref, f32[256,2048]{1,0:T(8,128)} %get-tuple-element.27.conv_ref, bf16[256,2048]{1,0:T(8,128)(2,1)} %query_ref.3), custom_call_target="tpu_custom_call" | custom-call | tf_op jit(solution)/shard_map/gate/pallas_call | solution.py:92
  210.1 9.6 %taps.1.refs_13_ = f32[128,128]{1,0:T(8,128)} custom-call(bf16[256,2048]{1,0:T(8,128)(2,1)} %get-tuple-element.29.grad_conv_ref, bf16[128,2048]{1,0:T(8,128)(2,1)} %collective-permute-done.rim_ref, bf16[256,2048]{1,0:T(8,128)(2,1)} %copy-done.9), custom_call_target="tpu_custom_call" | custom-call | tf_op jit(solution)/shard_map/taps/pallas_call | solution.py:142
  220.9 11.3 %weight.3.refs_1_ = bf16[1024,2048]{1,0:T(8,128)(2,1)} custom-call(bf16[256,2048]{1,0:T(8,128)(2,1)} %pick.5.refs_0_, bf16[256,2048]{1,0:T(8,128)(2,1)} %copy-done.6, bf16[256,2048]{1,0:T(8,128)(2,1)} %copy-done.7, bf16[256,2048]{1,0:T(8,128)(2,1)} %copy-done.10, bf16[256,2048]{1,0:T(8,128)(2,1)} %refs_4_.3, bf16[256,2048]{1,0:T(8,128)(2,1)} %once.7.refs_0_.refs_5_, ...), custom_call_target="tpu_custom_call" | custom-call | tf_op jit(solution)/shard_map/weight/pallas_call | solution.py:392
  235.7 6.7 %back.1 = (bf16[256,2048]{1,0:T(8,128)(2,1)}, bf16[256,2048]{1,0:T(8,128)(2,1)}) custom-call(f32[128,256]{1,0:T(8,128)} %get-tuple-element.36.base_ref, bf16[256,2048]{1,0:T(8,128)(2,1)} %get-tuple-element.29.grad_conv_ref, bf16[128,2048]{1,0:T(8,128)(2,1)} %copy-done.22, bf16[256,2048]{1,0:T(8,128)(2,1)} %key_ref.1, bf16[256,2048]{1,0:T(8,128)(2,1)} %value_ref.1, ...), custom_call_target="tpu_custom_call" | custom-call | tf_op jit(solution)/shard_map/back/pallas_call | solution.py:173
  244.6 2.9 %add_convert_fusion = bf16[256,2048]{1,0:T(8,128)(2,1)} fusion(bf16[256,2048]{1,0:T(8,128)(2,1)} %collective-permute-done.19, bf16[256,2048]{1,0:T(8,128)(2,1)S(1)} %copy-done.14, bf16[256,2048]{1,0:T(8,128)(2,1)S(1)} %copy-done.16, bf16[256,2048]{1,0:T(8,128)(2,1)S(1)} %copy-done.17), kind=kLoop, calls=%fused_computation | loop fusion | flops 4194304 | bytes 5242880 | tf_op jit(solution)/shard_map/convert_element_type | solution.py:450
  (119 shorter events, 51.9 us)
Async XLA Ops:
  0.6 10.8 %collective-permute-start.1 = (bf16[1024,2048]{1,0:T(8,128)(2,1)}, bf16[1024,2048]{1,0:T(8,128)(2,1)}, u32[]{:S(2)}, u32[]{:S(2)}) collective-permute-start(bf16[1024,2048]{1,0:T(8,128)(2,1)} %refs_2_.5), channel_id=1, source_target_pairs={{0,4},{4,0},{8,12},{12,8},{16,20},{20,16},{24,28},{28,24},{1,5},{5... | collective-permute-start | bytes 12582920 | tf_op jit(solution)/shard_map/ppermute | solution.py:201
  4.0 7.4 %collective-permute-start = (bf16[128,2048]{1,0:T(8,128)(2,1)}, bf16[128,2048]{1,0:T(8,128)(2,1)}, u32[]{:S(2)}, u32[]{:S(2)}) collective-permute-start(bf16[128,2048]{1,0:T(8,128)(2,1)} %slice.12), channel_id=1, source_target_pairs={{0,4},{4,8},{8,12},{12,16},{16,20},{20,24},{24,28},{1,5},{5,9},{9,... | collective-permute-start | bytes 1572872 | tf_op jit(solution)/shard_map/ppermute | solution.py:196
  6.7 26.1 %collective-permute-start.3 = (bf16[256,2048]{1,0:T(8,128)(2,1)}, bf16[256,2048]{1,0:T(8,128)(2,1)S(1)}, u32[]{:S(2)}, u32[]{:S(2)}) collective-permute-start(bf16[256,2048]{1,0:T(8,128)(2,1)} %refs_4_.3), channel_id=1, source_target_pairs={{0,8},{4,12},{8,0},{12,4},{16,24},{20,28},{24,16},{28,20},{1,9},{5... | collective-permute-start | bytes 3145736 | tf_op jit(solution)/shard_map/ppermute | solution.py:201
  9.0 29.5 %collective-permute-start.4 = (bf16[256,2048]{1,0:T(8,128)(2,1)}, bf16[256,2048]{1,0:T(8,128)(2,1)S(1)}, u32[]{:S(2)}, u32[]{:S(2)}) collective-permute-start(bf16[256,2048]{1,0:T(8,128)(2,1)} %refs_4_.3), channel_id=1, source_target_pairs={{0,16},{4,20},{8,24},{12,28},{16,0},{20,4},{24,8},{28,12},{1,17},{... | collective-permute-start | bytes 3145736 | tf_op jit(solution)/shard_map/ppermute | solution.py:201
  17.9 30.7 %collective-permute-start.2 = (bf16[256,2048]{1,0:T(8,128)(2,1)}, bf16[256,2048]{1,0:T(8,128)(2,1)S(1)}, u32[]{:S(2)}, u32[]{:S(2)}) collective-permute-start(bf16[256,2048]{1,0:T(8,128)(2,1)} %get-tuple-element.21.refs_3_.refs_0_), channel_id=1, source_target_pairs={{0,1},{1,2},{2,3},{3,0},{4,5},{5,6},{6,7},{7,4},{8,9},{9,10},{10,1... | collective-permute-start | bytes 3145736 | tf_op jit(solution)/shard_map/ppermute | solution.py:206
  49.6 31.6 %collective-permute-start.5 = (bf16[256,2048]{1,0:T(8,128)(2,1)}, bf16[256,2048]{1,0:T(8,128)(2,1)S(1)}, u32[]{:S(2)}, u32[]{:S(2)}) collective-permute-start(bf16[256,2048]{1,0:T(8,128)(2,1)} %once.9.refs_3_.refs_1_), channel_id=1, source_target_pairs={{0,1},{1,2},{2,3},{3,0},{4,5},{5,6},{6,7},{7,4},{8,9},{9,10},{10,1... | collective-permute-start | bytes 3145736 | tf_op jit(solution)/shard_map/ppermute | solution.py:206
  50.9 17.5 %collective-permute-start.6 = (bf16[128,2048]{1,0:T(8,128)(2,1)}, bf16[128,2048]{1,0:T(8,128)(2,1)S(1)}, u32[]{:S(2)}, u32[]{:S(2)}) collective-permute-start(bf16[128,2048]{1,0:T(8,128)(2,1)} %slice.13.refs_3_), channel_id=1, source_target_pairs={{0,16},{4,20},{8,24},{12,28},{16,0},{20,4},{24,8},{28,12},{1,17},{... | collective-permute-start | bytes 1572872 | tf_op jit(solution)/shard_map/ppermute | solution.py:201
  55.4 15.1 %collective-permute-start.7 = (bf16[128,2048]{1,0:T(8,128)(2,1)}, bf16[128,2048]{1,0:T(8,128)(2,1)S(1)}, u32[]{:S(2)}, u32[]{:S(2)}) collective-permute-start(bf16[128,2048]{1,0:T(8,128)(2,1)} %slice.14.refs_4_), channel_id=1, source_target_pairs={{0,8},{4,12},{8,0},{12,4},{16,24},{20,28},{24,16},{28,20},{1,9},{5... | collective-permute-start | bytes 1572872 | tf_op jit(solution)/shard_map/ppermute | solution.py:201
  56.5 36.5 %collective-permute-start.12 = (bf16[256,2048]{1,0:T(8,128)(2,1)}, bf16[256,2048]{1,0:T(8,128)(2,1)S(1)}, u32[]{:S(2)}, u32[]{:S(2)}) collective-permute-start(bf16[256,2048]{1,0:T(8,128)(2,1)} %product.7.refs_1_), channel_id=1, source_target_pairs={{0,8},{4,12},{8,0},{12,4},{16,24},{20,28},{24,16},{28,20},{1,9},{5... | collective-permute-start | bytes 3145736 | tf_op jit(solution)/shard_map/ppermute | solution.py:201
  64.7 28.2 %collective-permute-start.13 = (bf16[256,2048]{1,0:T(8,128)(2,1)}, bf16[256,2048]{1,0:T(8,128)(2,1)S(1)}, u32[]{:S(2)}, u32[]{:S(2)}) collective-permute-start(bf16[256,2048]{1,0:T(8,128)(2,1)} %product.8.refs_4_), channel_id=1, source_target_pairs={{0,16},{4,20},{8,24},{12,28},{16,0},{20,4},{24,8},{28,12},{1,17},{... | collective-permute-start | bytes 3145736 | tf_op jit(solution)/shard_map/ppermute | solution.py:201
  78.6 35.9 %collective-permute-start.14 = (bf16[256,2048]{1,0:T(8,128)(2,1)}, bf16[256,2048]{1,0:T(8,128)(2,1)}, u32[]{:S(2)}, u32[]{:S(2)}) collective-permute-start(bf16[256,2048]{1,0:T(8,128)(2,1)} %product.9.refs_1_), channel_id=1, source_target_pairs={{0,24},{4,28},{8,16},{12,20},{16,8},{20,12},{24,0},{28,4},{1,25},{... | collective-permute-start | bytes 3145736 | tf_op jit(solution)/shard_map/ppermute | solution.py:201
  82.2 36.2 %collective-permute-start.8 = (bf16[256,2048]{1,0:T(8,128)(2,1)}, bf16[256,2048]{1,0:T(8,128)(2,1)S(1)}, u32[]{:S(2)}, u32[]{:S(2)}) collective-permute-start(bf16[256,2048]{1,0:T(8,128)(2,1)} %once.10.refs_2_), channel_id=1, source_target_pairs={{0,1},{1,2},{2,3},{3,0},{4,5},{5,6},{6,7},{7,4},{8,9},{9,10},{10,1... | collective-permute-start | bytes 3145736 | tf_op jit(solution)/shard_map/ppermute | solution.py:206
  93.0 21.6 %copy-start.4 = (bf16[256,2048]{1,0:T(8,128)(2,1)}, bf16[256,2048]{1,0:T(8,128)(2,1)S(1)}, u32[]{:S(2)}) copy-start(bf16[256,2048]{1,0:T(8,128)(2,1)S(1)} %collective-permute-done.12.refs_1_) | copy-start | bytes 3145732
  93.0 21.6 %copy-start.5 = (bf16[256,2048]{1,0:T(8,128)(2,1)}, bf16[256,2048]{1,0:T(8,128)(2,1)S(1)}, u32[]{:S(2)}) copy-start(bf16[256,2048]{1,0:T(8,128)(2,1)S(1)} %collective-permute-done.13.refs_2_) | copy-start | bytes 3145732
  116.8 25.6 %collective-permute-start.15 = (bf16[256,2048]{1,0:T(8,128)(2,1)}, bf16[256,2048]{1,0:T(8,128)(2,1)S(1)}, u32[]{:S(2)}, u32[]{:S(2)}) collective-permute-start(bf16[256,2048]{1,0:T(8,128)(2,1)} %pick.9), channel_id=1, source_target_pairs={{0,1},{1,2},{2,3},{3,0},{4,5},{5,6},{6,7},{7,4},{8,9},{9,10},{10,1... | collective-permute-start | bytes 3145736 | tf_op jit(solution)/shard_map/ppermute | solution.py:206
  121.6 27.8 %collective-permute-start.9 = (bf16[256,2048]{1,0:T(8,128)(2,1)}, bf16[256,2048]{1,0:T(8,128)(2,1)S(1)}, u32[]{:S(2)}, u32[]{:S(2)}) collective-permute-start(bf16[256,2048]{1,0:T(8,128)(2,1)} %pick.7), channel_id=1, source_target_pairs={{0,8},{4,12},{8,0},{12,4},{16,24},{20,28},{24,16},{28,20},{1,9},{5... | collective-permute-start | bytes 3145736 | tf_op jit(solution)/shard_map/ppermute | solution.py:201
  124.7 24.8 %collective-permute-start.10 = (bf16[256,2048]{1,0:T(8,128)(2,1)}, bf16[256,2048]{1,0:T(8,128)(2,1)S(1)}, u32[]{:S(2)}, u32[]{:S(2)}) collective-permute-start(bf16[256,2048]{1,0:T(8,128)(2,1)} %pick.8), channel_id=1, source_target_pairs={{0,16},{4,20},{8,24},{12,28},{16,0},{20,4},{24,8},{28,12},{1,17},{... | collective-permute-start | bytes 3145736 | tf_op jit(solution)/shard_map/ppermute | solution.py:201
  146.1 24.9 %collective-permute-start.16 = (bf16[256,2048]{1,0:T(8,128)(2,1)}, bf16[256,2048]{1,0:T(8,128)(2,1)}, u32[]{:S(2)}, u32[]{:S(2)}) collective-permute-start(bf16[256,2048]{1,0:T(8,128)(2,1)} %add.91.refs_4_), channel_id=1, source_target_pairs={{0,1},{1,2},{2,3},{3,0},{4,5},{5,6},{6,7},{7,4},{8,9},{9,10},{10,1... | collective-permute-start | bytes 3145736 | tf_op jit(solution)/shard_map/ppermute | solution.py:206
  151.5 27.2 %collective-permute-start.11 = (bf16[256,2048]{1,0:T(8,128)(2,1)}, bf16[256,2048]{1,0:T(8,128)(2,1)S(1)}, u32[]{:S(2)}, u32[]{:S(2)}) collective-permute-start(bf16[256,2048]{1,0:T(8,128)(2,1)} %once.11), channel_id=1, source_target_pairs={{0,24},{4,28},{8,16},{12,20},{16,8},{20,12},{24,0},{28,4},{1,25},{... | collective-permute-start | bytes 3145736 | tf_op jit(solution)/shard_map/ppermute | solution.py:201
  162.2 37.1 %collective-permute-start.18 = (bf16[256,2048]{1,0:T(8,128)(2,1)}, bf16[256,2048]{1,0:T(8,128)(2,1)S(1)}, u32[]{:S(2)}, u32[]{:S(2)}) collective-permute-start(bf16[256,2048]{1,0:T(8,128)(2,1)} %get-tuple-element.24), channel_id=1, source_target_pairs={{0,16},{4,20},{8,24},{12,28},{16,0},{20,4},{24,8},{28,12},{1,17},{... | collective-permute-start | bytes 3145736 | tf_op jit(solution)/shard_map/ppermute | solution.py:201
  162.2 37.2 %collective-permute-start.17 = (bf16[256,2048]{1,0:T(8,128)(2,1)}, bf16[256,2048]{1,0:T(8,128)(2,1)S(1)}, u32[]{:S(2)}, u32[]{:S(2)}) collective-permute-start(bf16[256,2048]{1,0:T(8,128)(2,1)} %get-tuple-element.22.refs_5_.refs_4_), channel_id=1, source_target_pairs={{0,8},{4,12},{8,0},{12,4},{16,24},{20,28},{24,16},{28,20},{1,9},{5... | collective-permute-start | bytes 3145736 | tf_op jit(solution)/shard_map/ppermute | solution.py:201
  173.7 26.2 %collective-permute-start.20 = (bf16[256,2048]{1,0:T(8,128)(2,1)}, bf16[256,2048]{1,0:T(8,128)(2,1)}, u32[]{:S(2)}, u32[]{:S(2)}) collective-permute-start(bf16[256,2048]{1,0:T(8,128)(2,1)} %add.92.refs_5_.refs_10_), channel_id=1, source_target_pairs={{0,1},{1,2},{2,3},{3,0},{4,5},{5,6},{6,7},{7,4},{8,9},{9,10},{10,1... | collective-permute-start | bytes 3145736 | tf_op jit(solution)/shard_map/ppermute | solution.py:206
  198.8 10.0 %collective-permute-start.23 = (bf16[256,2048]{1,0:T(8,128)(2,1)}, bf16[256,2048]{1,0:T(8,128)(2,1)S(1)}, u32[]{:S(2)}, u32[]{:S(2)}) collective-permute-start(bf16[256,2048]{1,0:T(8,128)(2,1)} %get-tuple-element.26.refs_5_), channel_id=1, source_target_pairs={{0,4},{4,0},{8,12},{12,8},{16,20},{20,16},{24,28},{28,24},{1,5},{5... | collective-permute-start | bytes 3145736 | tf_op jit(solution)/shard_map/ppermute | solution.py:201
  198.8 21.0 %collective-permute-start.24 = (bf16[256,2048]{1,0:T(8,128)(2,1)}, bf16[256,2048]{1,0:T(8,128)(2,1)}, u32[]{:S(2)}, u32[]{:S(2)}) collective-permute-start(bf16[256,2048]{1,0:T(8,128)(2,1)} %get-tuple-element.31), channel_id=1, source_target_pairs={{0,4},{4,0},{8,12},{12,8},{16,20},{20,16},{24,28},{28,24},{1,5},{5... | collective-permute-start | bytes 3145736 | tf_op jit(solution)/shard_map/ppermute | solution.py:201
  199.3 21.6 %collective-permute-start.25 = (bf16[256,2048]{1,0:T(8,128)(2,1)}, bf16[256,2048]{1,0:T(8,128)(2,1)}, u32[]{:S(2)}, u32[]{:S(2)}) collective-permute-start(bf16[256,2048]{1,0:T(8,128)(2,1)} %get-tuple-element.32), channel_id=1, source_target_pairs={{0,4},{4,0},{8,12},{12,8},{16,20},{20,16},{24,28},{28,24},{1,5},{5... | collective-permute-start | bytes 3145736 | tf_op jit(solution)/shard_map/ppermute | solution.py:201
  199.4 21.5 %collective-permute-start.26 = (bf16[256,2048]{1,0:T(8,128)(2,1)}, bf16[256,2048]{1,0:T(8,128)(2,1)}, u32[]{:S(2)}, u32[]{:S(2)}) collective-permute-start(bf16[256,2048]{1,0:T(8,128)(2,1)} %get-tuple-element.33), channel_id=1, source_target_pairs={{0,4},{4,0},{8,12},{12,8},{16,20},{20,16},{24,28},{28,24},{1,5},{5... | collective-permute-start | bytes 3145736 | tf_op jit(solution)/shard_map/ppermute | solution.py:201
  199.8 44.7 %collective-permute-start.19 = (bf16[256,2048]{1,0:T(8,128)(2,1)}, bf16[256,2048]{1,0:T(8,128)(2,1)}, u32[]{:S(2)}, u32[]{:S(2)}) collective-permute-start(bf16[256,2048]{1,0:T(8,128)(2,1)} %get-tuple-element.25), channel_id=1, source_target_pairs={{0,24},{4,28},{8,16},{12,20},{16,8},{20,12},{24,0},{28,4},{1,25},{... | collective-permute-start | bytes 3145736 | tf_op jit(solution)/shard_map/ppermute | solution.py:201
  208.8 12.1 %copy-start.18 = (bf16[256,2048]{1,0:T(8,128)(2,1)}, bf16[256,2048]{1,0:T(8,128)(2,1)S(1)}, u32[]{:S(2)}) copy-start(bf16[256,2048]{1,0:T(8,128)(2,1)S(1)} %collective-permute-done.23.refs_9_) | copy-start | bytes 3145732
  208.8 26.1 %collective-permute-start.21 = (bf16[128,2048]{1,0:T(8,128)(2,1)}, bf16[128,2048]{1,0:T(8,128)(2,1)S(1)}, u32[]{:S(2)}, u32[]{:S(2)}) collective-permute-start(bf16[128,2048]{1,0:T(8,128)(2,1)} %get-tuple-element.30), channel_id=1, source_target_pairs={{4,0},{8,4},{12,8},{16,12},{20,16},{24,20},{28,24},{5,1},{9,5},{13... | collective-permute-start | bytes 1572872 | tf_op jit(solution)/shard_map/ppermute | solution.py:196
  219.8 12.4 %collective-permute-start.22 = (f32[128,128]{1,0:T(8,128)}, f32[128,128]{1,0:T(8,128)S(1)}, u32[]{:S(2)}, u32[]{:S(2)}) collective-permute-start(f32[128,128]{1,0:T(8,128)} %taps.1.refs_13_), channel_id=1, source_target_pairs={{0,4},{4,0},{8,12},{12,8},{16,20},{20,16},{24,28},{28,24},{1,5},{5... | collective-permute-start | bytes 196616 | tf_op jit(solution)/shard_map/ppermute | solution.py:201
  233.9 8.6 %collective-permute-start.27 = (f32[128,128]{1,0:T(8,128)S(1)}, f32[128,128]{1,0:T(8,128)S(1)}, u32[]{:S(2)}, u32[]{:S(2)}) collective-permute-start(f32[128,128]{1,0:T(8,128)S(1)} %add.85.refs_0_), channel_id=1, source_target_pairs={{0,8},{4,12},{8,0},{12,4},{16,24},{20,28},{24,16},{28,20},{1,9},{5... | collective-permute-start | bytes 196616 | tf_op jit(solution)/shard_map/ppermute | solution.py:201
  244.0 4.3 %collective-permute-start.28 = (f32[128,128]{1,0:T(8,128)S(1)}, f32[128,128]{1,0:T(8,128)S(1)}, u32[]{:S(2)}, u32[]{:S(2)}) collective-permute-start(f32[128,128]{1,0:T(8,128)S(1)} %add.86), channel_id=1, source_target_pairs={{0,16},{4,20},{8,24},{12,28},{16,0},{20,4},{24,8},{28,12},{1,17},{... | collective-permute-start | bytes 196616 | tf_op jit(solution)/shard_map/ppermute | solution.py:201
  (23 other events, 66.3 us)
